TPU v7x, 32 devices: a whole 2x2x4 slice. The times are simulated.
32 devices in a mesh: cuts: 4 (over z), group: 8 (over y, x, core).
Axes of the slice: x: 2, y: 2, z: 4, core: 2. Of those that a mesh axis runs over, the one named last changes fastest.
Arguments:
- radiation: float32 [32, 2, 128, 128], P(('cuts', 'group')), may hold values from -6 to 6
- phases: float32 [32, 16, 128], P(('cuts', 'group')), may hold values from -3.140625 to 3.140625
- energy: float32 [32, 16, 128], P(('cuts', 'group')), may hold values from -5 to 5
- pixels: int32 [32, 16, 128], P(('cuts', 'group')), may hold values from 0 to 16383
- destination: int32 [32, 16], P(('cuts', 'group')), may hold values from 0 to 3, as said below
- propagator: float32 [2, 128, 128], replicated, may hold values from -1 to 1
- transmit: float32 [2, 32], replicated, may hold values from -1 to 1
Outputs:
- radiation_out: float32 [32, 2, 128, 128], P(('cuts', 'group'))
Inputs may be any that keep to these rules, and one draw needn't show every extreme that they name: `destination`: the blocks of one slice go to exactly 2 different cuts, 8 blocks to each; in every draw some cut receives 8 blocks from every slice of the same position within a cut.
All inputs are finite; a program needn't handle non-finite values.
Results may differ from a plain program's by a relative error of at most 0.0011.
Values sent between devices are 32-bit elements; how exact they have to be, the bound alone decides.
No kernel may reach another device: no remote copies, remote signals or barrier semaphores. Data moves between devices by JAX's collectives and lax.ppermute only.
A program may use at most 64 MiB of HBM per device.

v0:
```python
import functools
import math

import jax
import jax.numpy as jnp
from jax import lax
from jax.experimental import pallas as pl
from jax.experimental.pallas import tpu as pltpu
from jax.sharding import PartitionSpec as P

KICK_RATE = 0.5
PHASE_RATE = 1.0
EMIT_RATE = 0.5

AXES = ("cuts", "group")
F32 = jnp.float32
BF16 = jnp.bfloat16
KINDS = 4
VMEM_LIMIT = 48 * 1024 * 1024
WHOLE_VMEM = 60 * 1024 * 1024


def dot(left, right, left_dim, right_dim):
    dims = (((left_dim,), (right_dim,)), ((), ()))
    return lax.dot_general(left, right, dims, preferred_element_type=F32)


def exact_dot(left, right):
    return jnp.dot(left, right, precision=lax.Precision.HIGHEST, preferred_element_type=F32)


def split(value):
    high = value.astype(BF16)
    return high, (value - high.astype(F32)).astype(BF16)


def diffract(real, imag, propagator):
    size = real.shape[0]
    prop_real, prop_imag = propagator[0], propagator[1]
    form = jnp.concatenate(
        [
            jnp.concatenate([prop_real, -prop_imag], axis=1),
            jnp.concatenate([prop_imag, prop_real], axis=1),
        ],
        axis=0,
    )
    form_high, form_low = split(form)
    high, low = split(jnp.concatenate([real, imag], axis=1))
    both = dot(jnp.concatenate([high, low], axis=0), form_high, 1, 1)
    right = both[:size] + both[size:] + dot(high, form_low, 1, 1)
    high, low = split(jnp.concatenate([right[:, :size], right[:, size:]], axis=0))
    both = dot(form_high, jnp.concatenate([high, low], axis=1), 1, 0)
    out = both[:, :size] + both[:, size:] + dot(form_low, high, 1, 0)
    return out[:size], out[size:]


def cells(pixels, grid):
    half = grid // 2
    shift = grid.bit_length() - 1
    if grid == 1 << shift:
        row, col = lax.shift_right_arithmetic(pixels, shift), pixels & (grid - 1)
    else:
        row, col = pixels // grid, pixels % grid
    right = col >= half
    place = jnp.where(pixels < 0, -1, jnp.where(right, row + grid, row))
    return place, jnp.where(right, col - half, col)


def swapped(value):
    half = value.shape[1] // 2
    return jnp.concatenate([value[:, half:], value[:, :half]], axis=1)


def fold(first, second):
    left = lax.broadcasted_iota(jnp.int32, first.shape, 1) < first.shape[1] // 2
    return jnp.where(left, first, swapped(second)), jnp.where(left, swapped(first), second)


def chunks(blocks):
    width = 2 if blocks % 2 == 0 else 1
    return [(start, width) for start in range(0, blocks, width)]


def lanes(array, start, width):
    return jnp.concatenate([array[start + k : start + k + 1] for k in range(width)], axis=1)


def hits(ids, span):
    return lax.broadcasted_iota(jnp.int32, (span, ids.shape[1]), 0) == ids


def one_hot(place, start, width, span):
    ids = lanes(place, start, width).astype(F32)
    rows = lax.broadcasted_iota(jnp.int32, (span, ids.shape[1]), 0).astype(F32)
    if span <= 256:
        ids, rows = ids.astype(BF16), rows.astype(BF16)
    one, zero = jnp.ones((), BF16), jnp.zeros((), BF16)
    return jnp.where(rows == ids, one, zero)


def kick(real, imag, phases, energy, pixels, read_ref, hot_ref=None):
    grid = real.shape[0]
    half = grid // 2
    blocks, size = phases.shape
    upper, lower = fold(real, imag)
    low = jnp.concatenate([upper, lower], axis=0).astype(BF16)
    place, col = cells(pixels, grid)
    for start, width in chunks(blocks):
        hot = one_hot(place, start, width, 2 * grid)
        if hot_ref is not None:
            hot_ref[:, start * size : (start + width) * size] = hot
        picked = dot(low, hot, 0, 0)
        col_hit = hits(lanes(col, start, width), half)
        for part in range(2):
            value = picked[part * half : (part + 1) * half]
            value = jnp.sum(jnp.where(col_hit, value, 0.0), axis=0, keepdims=True)
            for k in range(width):
                read_ref[part, start + k : start + k + 1, :] = value[:, k * size : (k + 1) * size]
    read_real = read_ref[0, :blocks, :]
    read_imag = read_ref[1, :blocks, :]
    energy = energy - KICK_RATE * (read_real * jnp.cos(phases) - read_imag * jnp.sin(phases))
    return phases + PHASE_RATE * energy, energy


def emit(real, imag, phases, pixels, hot_ref, spread_ref, filled):
    grid = real.shape[0]
    half = grid // 2
    blocks, size = phases.shape
    place, col = cells(pixels, grid)
    weight_real = jnp.cos(phases)
    weight_imag = -jnp.sin(phases)
    for start, width in chunks(blocks):
        where = slice(start * size, (start + width) * size)
        if not filled:
            hot_ref[:, where] = one_hot(place, start, width, 2 * grid)
        col_hit = hits(lanes(col, start, width), half)
        for part, weight in ((0, weight_real), (1, weight_imag)):
            value = jnp.where(col_hit, lanes(weight, start, width), 0.0)
            spread_ref[part * half : (part + 1) * half, where] = value.astype(BF16)
    span = blocks * size
    source = dot(hot_ref[:, :span], spread_ref[:, :span], 1, 1)
    source_real, source_imag = fold(source[:grid], source[grid:])
    return real + EMIT_RATE * source_real, imag + EMIT_RATE * source_imag


def position():
    return lax.axis_index("cuts") * lax.axis_size("group") + lax.axis_index("group")


def kept_unless(index):
    return jnp.where(position() == index, 0.0, 1.0).astype(F32)


def kick_kernel(field_hbm, phases_hbm, energy_hbm, pixels_hbm, dest_hbm, out, field, phases, energy, pixels, dest, read_ref, sems):
    blocks, size = phases.shape
    pairs = ((field_hbm, field), (pixels_hbm, pixels), (phases_hbm, phases), (energy_hbm, energy), (dest_hbm, dest))
    copies = [pltpu.make_async_copy(source, target, sems.at[k]) for k, (source, target) in enumerate(pairs)]
    for copy in copies:
        copy.start()
    for copy in copies:
        copy.wait()
    new_phases, new_energy = kick(field[0], field[1], phases[...], energy[...], pixels[...], read_ref)
    out[0:blocks, :] = new_phases
    out[blocks : 2 * blocks, :] = new_energy
    out[2 * blocks : 3 * blocks, :] = pixels[...].astype(F32)
    square = (blocks, blocks)
    own = lax.broadcasted_iota(jnp.int32, square, 0) == lax.broadcasted_iota(jnp.int32, square, 1)
    goals = jnp.where(own, jnp.broadcast_to(dest[0:1, :].astype(F32), square), 0.0)
    out[3 * blocks : 4 * blocks, :] = jnp.broadcast_to(jnp.sum(goals, axis=1, keepdims=True), (blocks, size))


def by_destination(kinds):
    goals = kinds[-1]
    blocks = goals.shape[0]
    place = lax.broadcasted_iota(jnp.int32, goals.shape, 0)
    rank = jnp.zeros(goals.shape, jnp.int32)
    for block in range(blocks):
        goal = goals[block : block + 1]
        ahead = (goal < goals) | ((goal == goals) & (place > block))
        rank = rank + jnp.where(ahead, 1, 0)
    ordered = [jnp.zeros(kind.shape, F32) for kind in kinds]
    for block in range(blocks):
        here = rank[block : block + 1] == place
        ordered = [jnp.where(here, kind[block : block + 1], old) for kind, old in zip(kinds, ordered)]
    return ordered


def lane_groups(values, shifts):
    size = values[0].shape[1]
    group = lax.broadcasted_iota(jnp.int32, values[0].shape, 1) // (size // len(values))
    joined_up = None
    for k, (value, shift) in enumerate(zip(values, shifts)):
        if shift % size:
            value = pltpu.roll(value, shift % size, axis=1)
        joined_up = value if joined_up is None else jnp.where(group == k, value, joined_up)
    return joined_up


def radiate_kernel(blocks, dropped, field, state, propagator, out, hot_ref, spread_ref):
    pixels = state[2 * blocks : 3 * blocks, :].astype(jnp.int32)
    real, imag = emit(field[0], field[1], state[0:blocks, :], pixels, hot_ref, spread_ref, False)
    real, imag = diffract(real, imag, propagator)
    keep = kept_unless(dropped)
    out[0] = real * keep
    out[1] = imag * keep


def second_kernel(count, rows, cap, field, state, propagator, out, *rest):
    sends = rest[:-3]
    read_ref, hot_ref, spread_ref = rest[-3:]
    blocks, size = state.shape[0] // 4, state.shape[1]
    real, imag = field[0], field[1]
    grid = real.shape[0]
    pixels = state[2 * blocks : 3 * blocks, :].astype(jnp.int32)
    phases, energy = kick(real, imag, state[0:blocks, :], state[blocks : 2 * blocks, :], pixels, read_ref, hot_ref)
    kinds = by_destination((phases, energy, state[2 * blocks : 3 * blocks, :], state[3 * blocks : 4 * blocks, :]))
    if rows:
        pieces = len(kinds)
        width = size // pieces
        for chunk in range(blocks // cap):
            parts = [kind[chunk * cap : (chunk + 1) * cap] for kind in kinds]
            for piece in range(pieces):
                row = lane_groups(parts, [(k - piece) * width for k in range(pieces)])
                out[pl.ds(piece * cap * 3 + 2, cap, stride=3), chunk, :] = row
    else:
        cuts = len(sends)
        cut = lax.div(lax.rem(position() + 1, count), count // cuts)
        for ahead, send in enumerate(sends):
            wanted = lax.rem(cut + ahead, cuts).astype(F32)
            chunk = [jnp.zeros((cap, size), F32)] * 2 + [jnp.full((cap, size), -1.0, F32)]
            for start in range(0, blocks, cap):
                goes = kinds[3][start : start + cap] == wanted
                chunk = [jnp.where(goes, kind[start : start + cap], old) for kind, old in zip(kinds, chunk)]
            for kind in range(3):
                send[kind * cap : (kind + 1) * cap, :] = chunk[kind]
    real, imag = emit(real, imag, phases, pixels, hot_ref, spread_ref, True)
    real, imag = diffract(real, imag, propagator)
    keep = kept_unless(count - 2)
    real, imag = real * keep, imag * keep
    if rows:
        for part in range(grid // rows):
            out[3 * part] = real[part * rows : (part + 1) * rows]
            out[3 * part + 1] = imag[part * rows : (part + 1) * rows]
    else:
        out[0] = real
        out[1] = imag


def matrix_kernel(transmit, cos_out, sin_out, cos_in, sin_in, out):
    gain_real, gain_imag = transmit[0:1, :], transmit[1:2, :]
    cosine, sine = cos_out[...], sin_out[...]
    real = cosine * gain_real - sine * gain_imag
    imag = cosine * gain_imag + sine * gain_real
    full_real = exact_dot(real, cos_in[...]) + exact_dot(imag, sin_in[...])
    full_imag = exact_dot(imag, cos_in[...]) - exact_dot(real, sin_in[...])
    form = jnp.concatenate(
        [
            jnp.concatenate([full_real, -full_imag], axis=1),
            jnp.concatenate([full_imag, full_real], axis=1),
        ],
        axis=0,
    )
    high, low = split(form)
    out[...] = jnp.concatenate([high, high, low], axis=1)


def filter_kernel(cuts, chunk_count, matrix, data, out):
    count = data.shape[0] // 3
    rows, size = data.shape[1:]
    groups = count // cuts
    stacked = jnp.concatenate(
        [
            jnp.concatenate([data[pl.ds(part, count, stride=3), j, :] for part in range(2)], axis=0)
            for j in range(rows)
        ],
        axis=1,
    )
    high, low = split(stacked)
    result = dot(matrix[...], jnp.concatenate([high, low, high], axis=0), 1, 0)
    for part in range(2):
        for j in range(rows):
            out[pl.ds(part, count, stride=3), j, :] = result[
                part * count : (part + 1) * count, j * size : (j + 1) * size
            ]
    bundles = [pltpu.roll(data[pl.ds(2, count, stride=3), chunk, :], 1, axis=0) for chunk in range(chunk_count)]
    goals = [bundle[:, size - 1 : size] for bundle in bundles]
    for cut in range(cuts):
        chosen = bundles[0]
        for bundle, goal in zip(bundles[1:], goals[1:]):
            chosen = jnp.where(goal == float(cut), bundle, chosen)
        first = cut * groups + 2
        fits = min(groups, count - first)
        for source in range(cuts):
            tile = chosen[source * groups : (source + 1) * groups]
            out[pl.ds(3 * first + 2, fits, stride=3), source, :] = tile[:fits]
            for k in range(fits, groups):
                out[3 * (first + k - count) + 2, source : source + 1, :] = tile[k : k + 1]


def joined(chunks_in):
    cap = chunks_in[0].shape[0] // 3
    kinds = [
        jnp.concatenate([chunk[kind * cap : (kind + 1) * cap, :] for chunk in chunks_in], axis=0)
        for kind in range(3)
    ]
    return kinds[0], kinds[1], kinds[2].astype(jnp.int32)


def relayed(fields, cuts):
    count = fields.shape[0] // 3
    size = fields.shape[2]
    width = size // KINDS
    bundles = [fields[pl.ds(2, count, stride=3), cut, :] for cut in range(cuts)]
    kinds = [lane_groups(bundles, [(cut - kind) * width for cut in range(cuts)]) for kind in range(KINDS)]
    wanted = lax.div(lax.rem(position() + (count - 2), count), count // cuts).astype(F32)
    return kinds[0], kinds[1], jnp.where(kinds[3] == wanted, kinds[2], -1.0).astype(jnp.int32)


def third_kernel(cuts, fields, *rest):
    out, state, read_ref = rest[-3:]
    chunks_in = rest[:-3]
    if chunks_in:
        phases, energy, pixels = joined(chunks_in)
        out[...] = fields[...]
    else:
        phases, energy, pixels = relayed(fields, cuts)
        rows = fields.shape[1]
        for part in range(fields.shape[0] // 3):
            for kind in range(2):
                out[kind, part * rows : (part + 1) * rows, :] = fields[3 * part + kind]
    phases, energy = kick(out[0], out[1], phases, energy, pixels, read_ref)
    blocks = phases.shape[0]
    state[0:blocks, :] = phases
    state[blocks : 2 * blocks, :] = energy
    state[2 * blocks : 3 * blocks, :] = pixels.astype(F32)


def fourth_kernel(field, state, propagator, out, read_ref, hot_ref, spread_ref):
    blocks = state.shape[0] // 3
    pixels = state[2 * blocks : 3 * blocks, :].astype(jnp.int32)
    real, imag = field[0], field[1]
    phases, _ = kick(real, imag, state[0:blocks, :], state[blocks : 2 * blocks, :], pixels, read_ref, hot_ref)
    real, imag = emit(real, imag, phases, pixels, hot_ref, spread_ref, True)
    real, imag = diffract(real, imag, propagator)
    keep = kept_unless(0)
    out[0] = real * keep
    out[1] = imag * keep


def call(kernel, out_shape, scratch, flops, args, memory=pltpu.VMEM, limit=VMEM_LIMIT):
    specs = [pl.BlockSpec(memory_space=memory)] * len(args)
    return pl.pallas_call(
        kernel,
        out_shape=out_shape,
        in_specs=specs,
        out_specs=jax.tree.map(lambda _: pl.BlockSpec(memory_space=pltpu.VMEM), out_shape),
        scratch_shapes=scratch,
        compiler_params=pltpu.CompilerParams(vmem_limit_bytes=limit),
        cost_estimate=pl.CostEstimate(flops=flops, bytes_accessed=1 << 19, transcendentals=0),
    )(*args)


def time_tables(count):
    times = jnp.arange(count, dtype=jnp.int32)
    cos_out, sin_out = angle_table((times + (count - 4)) % count, times, count)
    return (cos_out / count, sin_out / count, *angle_table(times, times, count))


def angle_table(first_ids, second_ids, total_slices):
    product = first_ids[:, None] * second_ids[None, :] % total_slices
    angle = product.astype(F32) * (2.0 * math.pi / total_slices)
    return jnp.cos(angle), jnp.sin(angle)


def filter_any(field, transmit, count):
    grid = field.shape[1]
    span = grid * grid
    share = -(-span // count)
    flat = jnp.pad(field.reshape(2, span), ((0, 0), (0, share * count - span)))
    parts = flat.reshape(2, count, share).transpose(1, 0, 2)
    got = lax.all_to_all(parts, AXES, split_axis=0, concat_axis=0, tiled=True)
    got = jnp.roll(got, 2, axis=0)
    real, imag = got[:, 0], got[:, 1]
    times = jnp.arange(count, dtype=jnp.int32)
    cosine, sine = angle_table(times, times, count)
    spec_real = exact_dot(cosine, real) + exact_dot(sine, imag)
    spec_imag = exact_dot(cosine, imag) - exact_dot(sine, real)
    gain_real, gain_imag = transmit[0][:, None], transmit[1][:, None]
    shaped_real = gain_real * spec_real - gain_imag * spec_imag
    shaped_imag = gain_real * spec_imag + gain_imag * spec_real
    back_real = (exact_dot(cosine, shaped_real) - exact_dot(sine, shaped_imag)) / count
    back_imag = (exact_dot(cosine, shaped_imag) + exact_dot(sine, shaped_real)) / count
    back = jnp.stack([back_real, back_imag], axis=1)
    sent = jnp.roll(back, 2, axis=0)
    fields = lax.all_to_all(sent, AXES, split_axis=0, concat_axis=0, tiled=True)
    fields = fields.transpose(1, 0, 2).reshape(2, share * count)[:, :span]
    return fields.reshape(2, grid, grid)


def on_device(radiation, phases, energy, pixels, destination, propagator, transmit):
    cuts, groups = lax.axis_size("cuts"), lax.axis_size("group")
    count = cuts * groups
    grid = radiation.shape[-1]
    blocks, size = phases.shape[1:]
    cap = max(2, 2 * blocks // cuts)
    rows = grid // count if grid % count == 0 else 0
    if rows != 4 or cap * KINDS != count or cuts != KINDS or size % 128 or blocks != 2 * cap or groups % 8:
        rows = 0
    field = radiation[0]
    shape = lambda *dims: jax.ShapeDtypeStruct(dims, F32)
    read = lambda number: pltpu.VMEM((2, number, size), F32)
    hot = lambda number: [pltpu.VMEM((2 * grid, number * size), BF16), pltpu.VMEM((grid, number * size), BF16)]
    pass_flops = 4 * blocks * size * grid * grid
    prop_flops = 48 * grid**3

    state = call(
        kick_kernel, shape(4 * blocks, size),
        [
            pltpu.VMEM((2, grid, grid), F32),
            pltpu.VMEM((blocks, size), F32),
            pltpu.VMEM((blocks, size), F32),
            pltpu.VMEM((blocks, size), jnp.int32),
            pltpu.VMEM((1, blocks), jnp.int32),
            read(blocks),
            pltpu.SemaphoreType.DMA((5,)),
        ],
        pass_flops, (field, phases[0], energy[0], pixels[0], destination), pl.ANY, WHOLE_VMEM,
    )
    route = [((i + 1) % count, i) for i in range(count)]
    behind = lax.ppermute(state, AXES, route)
    field = call(
        functools.partial(radiate_kernel, blocks, count - 1), shape(2, grid, grid), hot(blocks), pass_flops + prop_flops,
        (field, state, propagator),
    )
    part_shape = shape(count * 3, rows, grid) if rows else shape(2, grid, grid)
    send_shapes = [] if rows else [shape(3 * cap, size)] * cuts
    field, *sends = call(
        functools.partial(second_kernel, count, rows, cap), (part_shape, *send_shapes),
        [read(blocks)] + hot(blocks), 2 * pass_flops + prop_flops,
        (field, behind, propagator),
    )
    chunks_in = [
        lax.ppermute(send, AXES, [(i, (i + 3 + groups * ahead) % count) for i in range(count)])
        for ahead, send in enumerate(sends)
    ]
    if rows:
        matrix = call(
            matrix_kernel, jax.ShapeDtypeStruct((2 * count, 6 * count), BF16), [], 1 << 20,
            (transmit, *time_tables(count)),
        )
        data = lax.all_to_all(field, AXES, split_axis=0, concat_axis=0, tiled=True)
        sent = call(
            functools.partial(filter_kernel, cuts, blocks // cap), shape(count * 3, rows, grid), [], 1 << 24,
            (matrix, data),
        )
        fields = lax.all_to_all(sent, AXES, split_axis=0, concat_axis=0, tiled=True)
    else:
        fields = filter_any(field, transmit, count)
    capacity = cuts * cap
    share = capacity // blocks
    field, state = call(
        functools.partial(third_kernel, cuts), (shape(2, grid, grid), shape(3 * capacity, size)),
        [read(capacity)], share * pass_flops, (fields, *chunks_in),
    )
    behind = lax.ppermute(state, AXES, route)
    field = call(
        functools.partial(radiate_kernel, capacity, 1), shape(2, grid, grid), hot(capacity),
        share * pass_flops + prop_flops, (field, state, propagator),
    )
    out = call(
        fourth_kernel, shape(2, grid, grid), [read(capacity)] + hot(capacity),
        2 * share * pass_flops + prop_flops, (field, behind, propagator),
    )
    return out[None]


def solution(mesh):
    return jax.shard_map(
        on_device,
        mesh=mesh,
        in_specs=(
            P(("cuts", "group"), None, None, None),
            P(("cuts", "group"), None, None),
            P(("cuts", "group"), None, None),
            P(("cuts", "group"), None, None),
            P(("cuts", "group"), None),
            P(),
            P(),
        ),
        out_specs=P(("cuts", "group"), None, None, None),
        check_vma=False,
    )
```

profile of v0, /device:TPU:1, one launch (start us, length us, event | category | flops | bytes accessed | tf_op | source)
XLA Modules:
  0.0 46.1 jit_solution(13527370149752222619)
XLA Ops:
  0.0 0.0 copy-start.1
  0.0 0.0 copy-start.2
  0.0 2.1 %shard_map.74.state = f32[64,128]{1,0:T(8,128)} custom-call(f32[2,128,128]{2,1,0:T(8,128)} %bitcast.5, f32[16,128]{1,0:T(8,128)} %bitcast.7, f32[16,128]{1,0:T(8,128)} %bitcast.8, s32[16,128]{1,0:T(8,128)} %bitcast.9, s32[1,16]{1,0:T(1,128)} %dest_hbm.1), custom_call_target="tpu_custom_call" | custom-call | flops 134217728 | bytes 524288 | tf_op jit(solution)/shard_map/pallas_call | solution.py:352
  2.1 0.1 collective-permute-start
  2.2 0.0 copy-done.1
  2.2 0.0 copy-done.2
  2.2 0.0 copy-start.3
  2.2 0.8 %copy-done.3 = f32[64,128]{1,0:T(8,128)S(1)} copy-done((f32[64,128]{1,0:T(8,128)S(1)}, f32[64,128]{1,0:T(8,128)}, u32[]{:S(2)}) %copy-start.3) | copy-done | bytes 32792
  3.0 1.1 %shard_map.75.field = f32[2,128,128]{2,1,0:T(8,128)S(1)} custom-call(f32[2,128,128]{2,1,0:T(8,128)S(1)} %bitcast.6, f32[64,128]{1,0:T(8,128)S(1)} %copy-done.3, f32[2,128,128]{2,1,0:T(8,128)S(1)} %copy-done.2), custom_call_target="tpu_custom_call" | custom-call | flops 234881024 | bytes 524288 | tf_op jit(solution)/shard_map/pallas_call | solution.py:352
  4.1 2.5 %collective-permute-done.state = f32[64,128]{1,0:T(8,128)S(1)} collective-permute-done((f32[64,128]{1,0:T(8,128)}, f32[64,128]{1,0:T(8,128)S(1)}, u32[]{:S(2)}, u32[]{:S(2)}) %collective-permute-start) | collective-permute-done | bytes 32800 | tf_op jit(solution)/shard_map/ppermute | solution.py:430
  6.6 2.3 %shard_map.76 = f32[96,4,128]{2,1,0:T(4,128)} custom-call(f32[2,128,128]{2,1,0:T(8,128)S(1)} %shard_map.75.field, f32[64,128]{1,0:T(8,128)S(1)} %collective-permute-done.state, f32[2,128,128]{2,1,0:T(8,128)S(1)} %copy-done.2), custom_call_target="tpu_custom_call" | custom-call | flops 369098752 | bytes 524288 | tf_op jit(solution)/shard_map/pallas_call | solution.py:352
  8.8 9.3 %all-to-all-start = ((f32[96,4,128]{2,1,0:T(4,128)}), f32[96,4,128]{2,1,0:T(4,128)S(1)}, u32[]{:S(2)}, u32[]{:S(2)}) async-start(f32[96,4,128]{2,1,0:T(4,128)} %shard_map.76), calls=%async_computation | async-start | bytes 393216 | tf_op jit(solution)/shard_map/all_to_all | solution.py:451
  18.1 0.1 fusion.12
  18.2 0.2 sine_multiply_fusion
  18.4 0.0 copy-start
  18.4 0.7 %copy-done = f32[2,32]{1,0:T(2,128)S(1)} copy-done((f32[2,32]{1,0:T(2,128)S(1)}, f32[2,32]{1,0:T(2,128)}, u32[]{:S(2)}) %copy-start) | copy-done | bytes 280
  19.1 0.3 shard_map.73.matrix
  19.4 7.9 %all-to-all-done.data = f32[96,4,128]{2,1,0:T(4,128)S(1)} async-done(((f32[96,4,128]{2,1,0:T(4,128)}), f32[96,4,128]{2,1,0:T(4,128)S(1)}, u32[]{:S(2)}, u32[]{:S(2)}) %all-to-all-start) | async-done | bytes 196640 | tf_op jit(solution)/shard_map/all_to_all | solution.py:451
  27.3 0.3 shard_map.77
  27.6 11.4 %all_to_all.10.fields = f32[96,4,128]{2,1,0:T(4,128)S(1)} all-to-all(f32[96,4,128]{2,1,0:T(4,128)S(1)} %shard_map.77), channel_id=1, replica_groups=mesh['cuts'=4,'group'=8] {'cuts','group'}, dimensions={0} | all-to-all | bytes 393216 | tf_op jit(solution)/shard_map/all_to_all | solution.py:456
  39.0 0.8 %shard_map.78 = (f32[2,128,128]{2,1,0:T(8,128)S(1)}, f32[96,128]{1,0:T(8,128)S(1)}) custom-call(f32[96,4,128]{2,1,0:T(4,128)S(1)} %all_to_all.10.fields), custom_call_target="tpu_custom_call" | custom-call | flops 268435456 | bytes 524288 | tf_op jit(solution)/shard_map/pallas_call | solution.py:352
  39.8 0.1 collective-permute-start.1
  39.9 1.4 %shard_map.79.field = f32[2,128,128]{2,1,0:T(8,128)S(1)} custom-call(f32[2,128,128]{2,1,0:T(8,128)S(1)} %get-tuple-element.7.field, f32[96,128]{1,0:T(8,128)S(1)} %get-tuple-element.8.state, f32[2,128,128]{2,1,0:T(8,128)S(1)} %copy-done.2), custom_call_target="tpu_custom_call" | custom-call | flops 369098752 | bytes 524288 | tf_op jit(solution)/shard_map/pallas_call | solution.py:352
  41.3 2.1 %collective-permute-done.1.state = f32[96,128]{1,0:T(8,128)S(1)} collective-permute-done((f32[96,128]{1,0:T(8,128)S(1)}, f32[96,128]{1,0:T(8,128)S(1)}, u32[]{:S(2)}, u32[]{:S(2)}) %collective-permute-start.1) | collective-permute-done | bytes 49184 | tf_op jit(solution)/shard_map/ppermute | solution.py:465
  43.4 2.7 %shard_map.80 = f32[2,128,128]{2,1,0:T(8,128)} custom-call(f32[2,128,128]{2,1,0:T(8,128)S(1)} %shard_map.79.field, f32[96,128]{1,0:T(8,128)S(1)} %collective-permute-done.1.state, f32[2,128,128]{2,1,0:T(8,128)S(1)} %copy-done.2), custom_call_target="tpu_custom_call" | custom-call | flops 637534208 | bytes 524288 | tf_op jit(solution)/shard_map/pallas_call | solution.py:352
  (1 shorter events, 0.0 us)
Async XLA Ops:
  0.0 2.2 %copy-start.1 = (f32[1,2,128,128]{3,2,1,0:T(8,128)S(1)}, f32[1,2,128,128]{3,2,1,0:T(8,128)}, u32[]{:S(2)}) copy-start(f32[1,2,128,128]{3,2,1,0:T(8,128)} %param.7) | copy-start | bytes 393220
  0.0 2.2 %copy-start.2 = (f32[2,128,128]{2,1,0:T(8,128)S(1)}, f32[2,128,128]{2,1,0:T(8,128)}, u32[]{:S(2)}) copy-start(f32[2,128,128]{2,1,0:T(8,128)} %propagator.7) | copy-start | bytes 393220
  2.1 4.5 %collective-permute-start = (f32[64,128]{1,0:T(8,128)}, f32[64,128]{1,0:T(8,128)S(1)}, u32[]{:S(2)}, u32[]{:S(2)}) collective-permute-start(f32[64,128]{1,0:T(8,128)} %shard_map.74.state), channel_id=1, source_target_pairs={{1,0},{2,1},{3,2},{4,3},{5,4},{6,5},{7,6},{8,7},{9,8},{10,9},{11,1... | collective-permute-start | bytes 98312 | tf_op jit(solution)/shard_map/ppermute | solution.py:430
  2.2 0.8 %copy-start.3 = (f32[64,128]{1,0:T(8,128)S(1)}, f32[64,128]{1,0:T(8,128)}, u32[]{:S(2)}) copy-start(f32[64,128]{1,0:T(8,128)} %shard_map.74.state) | copy-start | bytes 98308
  8.8 18.5 %all-to-all-start = ((f32[96,4,128]{2,1,0:T(4,128)}), f32[96,4,128]{2,1,0:T(4,128)S(1)}, u32[]{:S(2)}, u32[]{:S(2)}) async-start(f32[96,4,128]{2,1,0:T(4,128)} %shard_map.76), calls=%async_computation | async-start | bytes 393216 | tf_op jit(solution)/shard_map/all_to_all | solution.py:451
  18.4 0.7 %copy-start = (f32[2,32]{1,0:T(2,128)S(1)}, f32[2,32]{1,0:T(2,128)}, u32[]{:S(2)}) copy-start(f32[2,32]{1,0:T(2,128)} %transmit.1) | copy-start | bytes 772
  39.8 3.6 %collective-permute-start.1 = (f32[96,128]{1,0:T(8,128)S(1)}, f32[96,128]{1,0:T(8,128)S(1)}, u32[]{:S(2)}, u32[]{:S(2)}) collective-permute-start(f32[96,128]{1,0:T(8,128)S(1)} %get-tuple-element.8.state), channel_id=1, source_target_pairs={{1,0},{2,1},{3,2},{4,3},{5,4},{6,5},{7,6},{8,7},{9,8},{10,9},{11,1... | collective-permute-start | bytes 147464 | tf_op jit(solution)/shard_map/ppermute | solution.py:465
where the time goes:
time: 46.4 us; the launch traced here: 46.1 us
  waiting for transfers between devices  12.5 us (27%)
  blocking collectives  11.4 us (25%)
  Pallas kernels  11.1 us (24%)
  starting transfers between devices  9.44 us (20%)
  local copies, waits for them, and re-layouts  1.44 us (3%)
    all_to_all x1, blocking collectives, on_device(): fields = lax.all_to_all(sent, AXES, split_axis=0, concat_axis=0, tiled=True)  11.4 us
    pallas_call x8, Pallas kernels, call(): pl.pallas_call(kernel, out_shape=out_shape, in_specs=specs, out_specs=jax...  11.1 us
    all_to_all x1, starting transfers between devices, on_device(): data = lax.all_to_all(field, AXES, split_axis=0, concat_axis=0, tiled=True)  9.28 us
    all_to_all x1, waiting for transfers between devices, on_device(): data = lax.all_to_all(field, AXES, split_axis=0, concat_axis=0, tiled=True)  7.94 us
    ppermute x2, waiting for transfers between devices, on_device(): behind = lax.ppermute(state, AXES, route)  4.52 us
    unnamed x8, local copies, waits for them, and re-layouts  1.44 us
  transfers between devices with their start and end apart: 3, of which 3 were waited for; matrix products, arithmetic and copies ran while one was open for 1% of the time, Pallas kernels for 6%

commit v1 on v0

--- a/solution.py
+++ b/solution.py
@@ -17,7 +17,6 @@
 BF16 = jnp.bfloat16
 KINDS = 4
 VMEM_LIMIT = 48 * 1024 * 1024
-WHOLE_VMEM = 60 * 1024 * 1024
 
 
 def dot(left, right, left_dim, right_dim):
@@ -34,8 +33,7 @@
     return high, (value - high.astype(F32)).astype(BF16)
 
 
-def diffract(real, imag, propagator):
-    size = real.shape[0]
+def real_form(propagator):
     prop_real, prop_imag = propagator[0], propagator[1]
     form = jnp.concatenate(
         [
@@ -44,7 +42,11 @@
         ],
         axis=0,
     )
-    form_high, form_low = split(form)
+    return split(form)
+
+
+def diffract(real, imag, form_high, form_low):
+    size = real.shape[0]
     high, low = split(jnp.concatenate([real, imag], axis=1))
     both = dot(jnp.concatenate([high, low], axis=0), form_high, 1, 1)
     right = both[:size] + both[size:] + dot(high, form_low, 1, 1)
@@ -196,16 +198,26 @@
     return joined_up
 
 
-def radiate_kernel(blocks, dropped, field, state, propagator, out, hot_ref, spread_ref):
+def radiate(blocks, dropped, field, state, form, out, hot_ref, spread_ref):
     pixels = state[2 * blocks : 3 * blocks, :].astype(jnp.int32)
     real, imag = emit(field[0], field[1], state[0:blocks, :], pixels, hot_ref, spread_ref, False)
-    real, imag = diffract(real, imag, propagator)
+    real, imag = diffract(real, imag, *form)
     keep = kept_unless(dropped)
     out[0] = real * keep
     out[1] = imag * keep
 
 
-def second_kernel(count, rows, cap, field, state, propagator, out, *rest):
+def first_radiate_kernel(blocks, dropped, field, state, propagator, out, high, low, hot_ref, spread_ref):
+    form = real_form(propagator)
+    high[...], low[...] = form
+    radiate(blocks, dropped, field, state, form, out, hot_ref, spread_ref)
+
+
+def radiate_kernel(blocks, dropped, field, state, high, low, out, hot_ref, spread_ref):
+    radiate(blocks, dropped, field, state, (high[...], low[...]), out, hot_ref, spread_ref)
+
+
+def second_kernel(count, rows, cap, field, state, high, low, out, *rest):
     sends = rest[:-3]
     read_ref, hot_ref, spread_ref = rest[-3:]
     blocks, size = state.shape[0] // 4, state.shape[1]
@@ -234,7 +246,7 @@
             for kind in range(3):
                 send[kind * cap : (kind + 1) * cap, :] = chunk[kind]
     real, imag = emit(real, imag, phases, pixels, hot_ref, spread_ref, True)
-    real, imag = diffract(real, imag, propagator)
+    real, imag = diffract(real, imag, high[...], low[...])
     keep = kept_unless(count - 2)
     real, imag = real * keep, imag * keep
     if rows:
@@ -335,19 +347,19 @@
     state[2 * blocks : 3 * blocks, :] = pixels.astype(F32)
 
 
-def fourth_kernel(field, state, propagator, out, read_ref, hot_ref, spread_ref):
+def fourth_kernel(field, state, high, low, out, read_ref, hot_ref, spread_ref):
     blocks = state.shape[0] // 3
     pixels = state[2 * blocks : 3 * blocks, :].astype(jnp.int32)
     real, imag = field[0], field[1]
     phases, _ = kick(real, imag, state[0:blocks, :], state[blocks : 2 * blocks, :], pixels, read_ref, hot_ref)
     real, imag = emit(real, imag, phases, pixels, hot_ref, spread_ref, True)
-    real, imag = diffract(real, imag, propagator)
+    real, imag = diffract(real, imag, high[...], low[...])
     keep = kept_unless(0)
     out[0] = real * keep
     out[1] = imag * keep
 
 
-def call(kernel, out_shape, scratch, flops, args, memory=pltpu.VMEM, limit=VMEM_LIMIT):
+def call(kernel, out_shape, scratch, flops, args, memory=pltpu.VMEM):
     specs = [pl.BlockSpec(memory_space=memory)] * len(args)
     return pl.pallas_call(
         kernel,
@@ -355,7 +367,7 @@
         in_specs=specs,
         out_specs=jax.tree.map(lambda _: pl.BlockSpec(memory_space=pltpu.VMEM), out_shape),
         scratch_shapes=scratch,
-        compiler_params=pltpu.CompilerParams(vmem_limit_bytes=limit),
+        compiler_params=pltpu.CompilerParams(vmem_limit_bytes=VMEM_LIMIT),
         cost_estimate=pl.CostEstimate(flops=flops, bytes_accessed=1 << 19, transcendentals=0),
     )(*args)
 
@@ -413,6 +425,7 @@
     pass_flops = 4 * blocks * size * grid * grid
     prop_flops = 48 * grid**3
 
+    given = (field, phases[0], energy[0], pixels[0], destination)
     state = call(
         kick_kernel, shape(4 * blocks, size),
         [
@@ -424,12 +437,14 @@
             read(blocks),
             pltpu.SemaphoreType.DMA((5,)),
         ],
-        pass_flops, (field, phases[0], energy[0], pixels[0], destination), pl.ANY, WHOLE_VMEM,
+        pass_flops, tuple(pltpu.with_memory_space_constraint(value, pltpu.HBM) for value in given), pl.ANY,
     )
     route = [((i + 1) % count, i) for i in range(count)]
     behind = lax.ppermute(state, AXES, route)
-    field = call(
-        functools.partial(radiate_kernel, blocks, count - 1), shape(2, grid, grid), hot(blocks), pass_flops + prop_flops,
+    form_shape = jax.ShapeDtypeStruct((2 * grid, 2 * grid), BF16)
+    field, *form = call(
+        functools.partial(first_radiate_kernel, blocks, count - 1),
+        (shape(2, grid, grid), form_shape, form_shape), hot(blocks), pass_flops + prop_flops,
         (field, state, propagator),
     )
     part_shape = shape(count * 3, rows, grid) if rows else shape(2, grid, grid)
@@ -437,7 +452,7 @@
     field, *sends = call(
         functools.partial(second_kernel, count, rows, cap), (part_shape, *send_shapes),
         [read(blocks)] + hot(blocks), 2 * pass_flops + prop_flops,
-        (field, behind, propagator),
+        (field, behind, *form),
     )
     chunks_in = [
         lax.ppermute(send, AXES, [(i, (i + 3 + groups * ahead) % count) for i in range(count)])
@@ -465,11 +480,11 @@
     behind = lax.ppermute(state, AXES, route)
     field = call(
         functools.partial(radiate_kernel, capacity, 1), shape(2, grid, grid), hot(capacity),
-        share * pass_flops + prop_flops, (field, state, propagator),
+        share * pass_flops + prop_flops, (field, state, *form),
     )
     out = call(
         fourth_kernel, shape(2, grid, grid), [read(capacity)] + hot(capacity),
-        2 * share * pass_flops + prop_flops, (field, behind, propagator),
+        2 * share * pass_flops + prop_flops, (field, behind, *form),
     )
     return out[None]
 

time: 46.4 us -> 45.5 us (0.981)
  local copies, waits for them, and re-layouts: 1.44 us -> 0.68 us
  Pallas kernels: 11.1 us -> 10.5 us
  waiting for transfers between devices: 12.5 us -> 13 us
    unnamed x8 -> x6, local copies, waits for them, and re-layouts: 1.44 us -> 0.68 us
    pallas_call x8, Pallas kernels: 11.1 us -> 10.5 us  [call(): pl.pallas_call(kernel, out_shape=out_shape, in_specs=specs, out_specs=jax...]
    ppermute x2, waiting for transfers between devices: 4.52 us -> 5.08 us  [on_device(): behind = lax.ppermute(state, AXES, route)]
where the time goes in v1:
time: 45.5 us; the launch traced here: 45.3 us
  waiting for transfers between devices  13 us (29%)
  blocking collectives  11.4 us (25%)
  Pallas kernels  10.5 us (23%)
  starting transfers between devices  9.43 us (21%)
  local copies, waits for them, and re-layouts  0.68 us (1%)
    all_to_all x1, blocking collectives, on_device(): fields = lax.all_to_all(sent, AXES, split_axis=0, concat_axis=0, tiled=True)  11.4 us
    pallas_call x8, Pallas kernels, call(): pl.pallas_call(kernel, out_shape=out_shape, in_specs=specs, out_specs=jax...  10.5 us
    all_to_all x1, starting transfers between devices, on_device(): data = lax.all_to_all(field, AXES, split_axis=0, concat_axis=0, tiled=True)  9.27 us
    all_to_all x1, waiting for transfers between devices, on_device(): data = lax.all_to_all(field, AXES, split_axis=0, concat_axis=0, tiled=True)  7.94 us
    ppermute x2, waiting for transfers between devices, on_device(): behind = lax.ppermute(state, AXES, route)  5.08 us
  transfers between devices with their start and end apart: 3, of which 3 were waited for; matrix products, arithmetic and copies ran while one was open for 1% of the time, Pallas kernels for 6%

profile of v1, /device:TPU:1, one launch (start us, length us, event | category | flops | bytes accessed | tf_op | source)
XLA Modules:
  0.0 45.3 jit_solution(5423732604975233206)
XLA Ops:
  0.0 0.0 copy-start.1
  0.0 0.0 copy-start.2
  0.0 1.5 %shard_map.74.state = f32[64,128]{1,0:T(8,128)S(1)} custom-call(f32[2,128,128]{2,1,0:T(8,128)} %bitcast.5, f32[16,128]{1,0:T(8,128)} %bitcast.7, f32[16,128]{1,0:T(8,128)} %bitcast.8, s32[16,128]{1,0:T(8,128)} %bitcast.9, s32[1,16]{1,0:T(1,128)} %dest_hbm.1), custom_call_target="tpu_custom_call" | custom-call | flops 134217728 | bytes 524288 | tf_op jit(solution)/shard_map/pallas_call | solution.py:364
  1.5 0.1 collective-permute-start
  1.6 0.0 copy-done.1
  1.6 0.0 copy-done.2
  1.6 1.1 %shard_map.75 = (f32[2,128,128]{2,1,0:T(8,128)S(1)}, bf16[256,256]{1,0:T(8,128)(2,1)S(1)}, bf16[256,256]{1,0:T(8,128)(2,1)S(1)}) custom-call(f32[2,128,128]{2,1,0:T(8,128)S(1)} %bitcast.6, f32[64,128]{1,0:T(8,128)S(1)} %shard_map.74.state, f32[2,128,128]{2,1,0:T(8,128)S(1)} %copy-done.2), custom_call_target="tpu_custom_call" | custom-call | flops 234881024 | bytes 524288 | tf_op jit(solution)/shard_map/pallas_call | solution.py:364
  2.7 3.0 %collective-permute-done.state = f32[64,128]{1,0:T(8,128)S(1)} collective-permute-done((f32[64,128]{1,0:T(8,128)S(1)}, f32[64,128]{1,0:T(8,128)S(1)}, u32[]{:S(2)}, u32[]{:S(2)}) %collective-permute-start) | collective-permute-done | bytes 32800 | tf_op jit(solution)/shard_map/ppermute | solution.py:443
  5.8 2.3 %shard_map.76 = f32[96,4,128]{2,1,0:T(4,128)} custom-call(f32[2,128,128]{2,1,0:T(8,128)S(1)} %get-tuple-element.10.field, f32[64,128]{1,0:T(8,128)S(1)} %collective-permute-done.state, bf16[256,256]{1,0:T(8,128)(2,1)S(1)} %get-tuple-element.11.high, bf16[256,256]{1,0:T(8,128)(2,1)S(1)} %get-tuple-element.12.low), custom_call_target="tpu_custom_call" | custom-call | flops 369098752 | bytes 524288 | tf_op jit(solution)/shard_map/pallas_call | solution.py:364
  8.0 9.3 %all-to-all-start = ((f32[96,4,128]{2,1,0:T(4,128)}), f32[96,4,128]{2,1,0:T(4,128)S(1)}, u32[]{:S(2)}, u32[]{:S(2)}) async-start(f32[96,4,128]{2,1,0:T(4,128)} %shard_map.76), calls=%async_computation | async-start | bytes 393216 | tf_op jit(solution)/shard_map/all_to_all | solution.py:466
  17.3 0.1 fusion.12
  17.4 0.2 sine_multiply_fusion
  17.5 0.0 copy-start
  17.6 0.7 %copy-done = f32[2,32]{1,0:T(2,128)S(1)} copy-done((f32[2,32]{1,0:T(2,128)S(1)}, f32[2,32]{1,0:T(2,128)}, u32[]{:S(2)}) %copy-start) | copy-done | bytes 280
  18.2 0.3 shard_map.73.matrix
  18.6 7.9 %all-to-all-done.data = f32[96,4,128]{2,1,0:T(4,128)S(1)} async-done(((f32[96,4,128]{2,1,0:T(4,128)}), f32[96,4,128]{2,1,0:T(4,128)S(1)}, u32[]{:S(2)}, u32[]{:S(2)}) %all-to-all-start) | async-done | bytes 196640 | tf_op jit(solution)/shard_map/all_to_all | solution.py:466
  26.5 0.3 shard_map.77
  26.8 11.4 %all_to_all.10.fields = f32[96,4,128]{2,1,0:T(4,128)S(1)} all-to-all(f32[96,4,128]{2,1,0:T(4,128)S(1)} %shard_map.77), channel_id=1, replica_groups=mesh['cuts'=4,'group'=8] {'cuts','group'}, dimensions={0} | all-to-all | bytes 393216 | tf_op jit(solution)/shard_map/all_to_all | solution.py:471
  38.2 0.8 %shard_map.78 = (f32[2,128,128]{2,1,0:T(8,128)S(1)}, f32[96,128]{1,0:T(8,128)S(1)}) custom-call(f32[96,4,128]{2,1,0:T(4,128)S(1)} %all_to_all.10.fields), custom_call_target="tpu_custom_call" | custom-call | flops 268435456 | bytes 524288 | tf_op jit(solution)/shard_map/pallas_call | solution.py:364
  39.0 0.1 collective-permute-start.1
  39.1 1.4 %shard_map.79.field = f32[2,128,128]{2,1,0:T(8,128)S(1)} custom-call(f32[2,128,128]{2,1,0:T(8,128)S(1)} %get-tuple-element.13.field, f32[96,128]{1,0:T(8,128)S(1)} %get-tuple-element.14.state, bf16[256,256]{1,0:T(8,128)(2,1)S(1)} %get-tuple-element.11.high, bf16[256,256]{1,0:T(8,128)(2,1)S(1)} %get-tuple-element.12.low), custom_call_target="tpu_custom_call" | custom-call | flops 369098752 | bytes 524288 | tf_op jit(solution)/shard_map/pallas_call | solution.py:364
  40.5 2.1 %collective-permute-done.1.state = f32[96,128]{1,0:T(8,128)S(1)} collective-permute-done((f32[96,128]{1,0:T(8,128)S(1)}, f32[96,128]{1,0:T(8,128)S(1)}, u32[]{:S(2)}, u32[]{:S(2)}) %collective-permute-start.1) | collective-permute-done | bytes 49184 | tf_op jit(solution)/shard_map/ppermute | solution.py:480
  42.6 2.7 %shard_map.80 = f32[2,128,128]{2,1,0:T(8,128)} custom-call(f32[2,128,128]{2,1,0:T(8,128)S(1)} %shard_map.79.field, f32[96,128]{1,0:T(8,128)S(1)} %collective-permute-done.1.state, bf16[256,256]{1,0:T(8,128)(2,1)S(1)} %get-tuple-element.11.high, bf16[256,256]{1,0:T(8,128)(2,1)S(1)} %get-tuple-element.12.low), custom_call_target="tpu_custom_call" | custom-call | flops 637534208 | bytes 524288 | tf_op jit(solution)/shard_map/pallas_call | solution.py:364
  (1 shorter events, 0.0 us)
Async XLA Ops:
  0.0 1.6 %copy-start.1 = (f32[1,2,128,128]{3,2,1,0:T(8,128)S(1)}, f32[1,2,128,128]{3,2,1,0:T(8,128)}, u32[]{:S(2)}) copy-start(f32[1,2,128,128]{3,2,1,0:T(8,128)} %param.7) | copy-start | bytes 393220
  0.0 1.6 %copy-start.2 = (f32[2,128,128]{2,1,0:T(8,128)S(1)}, f32[2,128,128]{2,1,0:T(8,128)}, u32[]{:S(2)}) copy-start(f32[2,128,128]{2,1,0:T(8,128)} %propagator.1) | copy-start | bytes 393220
  1.5 4.3 %collective-permute-start = (f32[64,128]{1,0:T(8,128)S(1)}, f32[64,128]{1,0:T(8,128)S(1)}, u32[]{:S(2)}, u32[]{:S(2)}) collective-permute-start(f32[64,128]{1,0:T(8,128)S(1)} %shard_map.74.state), channel_id=1, source_target_pairs={{1,0},{2,1},{3,2},{4,3},{5,4},{6,5},{7,6},{8,7},{9,8},{10,9},{11,1... | collective-permute-start | bytes 98312 | tf_op jit(solution)/shard_map/ppermute | solution.py:443
  8.0 18.5 %all-to-all-start = ((f32[96,4,128]{2,1,0:T(4,128)}), f32[96,4,128]{2,1,0:T(4,128)S(1)}, u32[]{:S(2)}, u32[]{:S(2)}) async-start(f32[96,4,128]{2,1,0:T(4,128)} %shard_map.76), calls=%async_computation | async-start | bytes 393216 | tf_op jit(solution)/shard_map/all_to_all | solution.py:466
  17.5 0.7 %copy-start = (f32[2,32]{1,0:T(2,128)S(1)}, f32[2,32]{1,0:T(2,128)}, u32[]{:S(2)}) copy-start(f32[2,32]{1,0:T(2,128)} %transmit.1) | copy-start | bytes 772
  39.0 3.6 %collective-permute-start.1 = (f32[96,128]{1,0:T(8,128)S(1)}, f32[96,128]{1,0:T(8,128)S(1)}, u32[]{:S(2)}, u32[]{:S(2)}) collective-permute-start(f32[96,128]{1,0:T(8,128)S(1)} %get-tuple-element.14.state), channel_id=1, source_target_pairs={{1,0},{2,1},{3,2},{4,3},{5,4},{6,5},{7,6},{8,7},{9,8},{10,9},{11,1... | collective-permute-start | bytes 147464 | tf_op jit(solution)/shard_map/ppermute | solution.py:480

commit v2 on v1

--- a/solution.py
+++ b/solution.py
@@ -207,7 +207,13 @@
     out[1] = imag * keep
 
 
-def first_radiate_kernel(blocks, dropped, field, state, propagator, out, high, low, hot_ref, spread_ref):
+def first_radiate_kernel(blocks, dropped, field, state, propagator, *rest):
+    *rest, hot_ref, spread_ref = rest
+    if len(rest) > 3:
+        *tables, out, high, low, matrix = rest
+        matrix[...] = filter_matrix(*tables)
+    else:
+        out, high, low = rest
     form = real_form(propagator)
     high[...], low[...] = form
     radiate(blocks, dropped, field, state, form, out, hot_ref, spread_ref)
@@ -227,13 +233,14 @@
     phases, energy = kick(real, imag, state[0:blocks, :], state[blocks : 2 * blocks, :], pixels, read_ref, hot_ref)
     kinds = by_destination((phases, energy, state[2 * blocks : 3 * blocks, :], state[3 * blocks : 4 * blocks, :]))
     if rows:
-        pieces = len(kinds)
+        pairs, pieces = rows // 2, len(kinds)
+        tiles = 2 * pairs + 1
         width = size // pieces
         for chunk in range(blocks // cap):
             parts = [kind[chunk * cap : (chunk + 1) * cap] for kind in kinds]
             for piece in range(pieces):
                 row = lane_groups(parts, [(k - piece) * width for k in range(pieces)])
-                out[pl.ds(piece * cap * 3 + 2, cap, stride=3), chunk, :] = row
+                out[pl.ds((piece * cap + 1) * tiles - 1, cap, stride=tiles), chunk, :] = row
     else:
         cuts = len(sends)
         cut = lax.div(lax.rem(position() + 1, count), count // cuts)
@@ -251,14 +258,16 @@
     real, imag = real * keep, imag * keep
     if rows:
         for part in range(grid // rows):
-            out[3 * part] = real[part * rows : (part + 1) * rows]
-            out[3 * part + 1] = imag[part * rows : (part + 1) * rows]
+            for pair in range(pairs):
+                first = part * rows + 2 * pair
+                out[part * tiles + pair] = real[first : first + 2]
+                out[part * tiles + pairs + pair] = imag[first : first + 2]
     else:
         out[0] = real
         out[1] = imag
 
 
-def matrix_kernel(transmit, cos_out, sin_out, cos_in, sin_in, out):
+def filter_matrix(transmit, cos_out, sin_out, cos_in, sin_in):
     gain_real, gain_imag = transmit[0:1, :], transmit[1:2, :]
     cosine, sine = cos_out[...], sin_out[...]
     real = cosine * gain_real - sine * gain_imag
@@ -273,16 +282,20 @@
         axis=0,
     )
     high, low = split(form)
-    out[...] = jnp.concatenate([high, high, low], axis=1)
+    return jnp.concatenate([high, high, low], axis=1)
 
 
 def filter_kernel(cuts, chunk_count, matrix, data, out):
-    count = data.shape[0] // 3
-    rows, size = data.shape[1:]
+    count = out.shape[0] // 3
+    rows, size = out.shape[1:]
     groups = count // cuts
+    pairs = rows // 2
+    tiles = 2 * pairs + 1
     stacked = jnp.concatenate(
         [
-            jnp.concatenate([data[pl.ds(part, count, stride=3), j, :] for part in range(2)], axis=0)
+            jnp.concatenate(
+                [data[pl.ds(part * pairs + j // 2, count, stride=tiles), j % 2, :] for part in range(2)], axis=0
+            )
             for j in range(rows)
         ],
         axis=1,
@@ -294,7 +307,10 @@
             out[pl.ds(part, count, stride=3), j, :] = result[
                 part * count : (part + 1) * count, j * size : (j + 1) * size
             ]
-    bundles = [pltpu.roll(data[pl.ds(2, count, stride=3), chunk, :], 1, axis=0) for chunk in range(chunk_count)]
+    bundles = [
+        pltpu.roll(data[pl.ds(tiles - 1, count, stride=tiles), chunk, :], 1, axis=0)
+        for chunk in range(chunk_count)
+    ]
     goals = [bundle[:, size - 1 : size] for bundle in bundles]
     for cut in range(cuts):
         chosen = bundles[0]
@@ -442,12 +458,18 @@
     route = [((i + 1) % count, i) for i in range(count)]
     behind = lax.ppermute(state, AXES, route)
     form_shape = jax.ShapeDtypeStruct((2 * grid, 2 * grid), BF16)
+    made = [shape(2, grid, grid), form_shape, form_shape]
+    tables = ()
+    if rows:
+        made.append(jax.ShapeDtypeStruct((2 * count, 6 * count), BF16))
+        tables = (transmit, *time_tables(count))
     field, *form = call(
-        functools.partial(first_radiate_kernel, blocks, count - 1),
-        (shape(2, grid, grid), form_shape, form_shape), hot(blocks), pass_flops + prop_flops,
-        (field, state, propagator),
-    )
-    part_shape = shape(count * 3, rows, grid) if rows else shape(2, grid, grid)
+        functools.partial(first_radiate_kernel, blocks, count - 1), made, hot(blocks), pass_flops + prop_flops,
+        (field, state, propagator, *tables),
+    )
+    matrix = form[2:]
+    form = form[:2]
+    part_shape = shape(count * (rows + 1), 2, grid) if rows else shape(2, grid, grid)
     send_shapes = [] if rows else [shape(3 * cap, size)] * cuts
     field, *sends = call(
         functools.partial(second_kernel, count, rows, cap), (part_shape, *send_shapes),
@@ -459,14 +481,10 @@
         for ahead, send in enumerate(sends)
     ]
     if rows:
-        matrix = call(
-            matrix_kernel, jax.ShapeDtypeStruct((2 * count, 6 * count), BF16), [], 1 << 20,
-            (transmit, *time_tables(count)),
-        )
         data = lax.all_to_all(field, AXES, split_axis=0, concat_axis=0, tiled=True)
         sent = call(
             functools.partial(filter_kernel, cuts, blocks // cap), shape(count * 3, rows, grid), [], 1 << 24,
-            (matrix, data),
+            (*matrix, data),
         )
         fields = lax.all_to_all(sent, AXES, split_axis=0, concat_axis=0, tiled=True)
     else:

time: 45.5 us -> 43.9 us (0.965)
  blocking collectives: 11.4 us -> 29 us
  starting transfers between devices: 9.43 us -> 0.16 us
  waiting for transfers between devices: 13 us -> 4.08 us
  Pallas kernels: 10.5 us -> 9.49 us
    all_to_all x0 -> x1, blocking collectives: none -> 17.8 us  [on_device(): data = lax.all_to_all(field, AXES, split_axis=0, concat_axis=0, tiled=True)]
    all_to_all x1 -> x0, starting transfers between devices: 9.27 us -> none  [on_device(): data = lax.all_to_all(field, AXES, split_axis=0, concat_axis=0, tiled=True)]
    all_to_all x1 -> x0, waiting for transfers between devices: 7.94 us -> none  [on_device(): data = lax.all_to_all(field, AXES, split_axis=0, concat_axis=0, tiled=True)]
    ppermute x2, waiting for transfers between devices: 5.08 us -> 4.08 us  [on_device(): behind = lax.ppermute(state, AXES, route)]
    pallas_call x8 -> x7, Pallas kernels: 10.5 us -> 9.49 us  [call(): pl.pallas_call(kernel, out_shape=out_shape, in_specs=specs, out_specs=jax...]
  transfers between devices with their start and end apart: 3 -> 2, of which waited for: 3 -> 2; matrix products, arithmetic and copies ran while one was open for 1% -> 1% of each run, Pallas kernels for 6% -> 6%
where the time goes in v2:
time: 43.9 us; the launch traced here: 43.8 us
  blocking collectives  29 us (66%)
  Pallas kernels  9.49 us (22%)
  waiting for transfers between devices  4.08 us (9%)
  local copies, waits for them, and re-layouts  0.66 us (2%)
    all_to_all x1, blocking collectives, on_device(): data = lax.all_to_all(field, AXES, split_axis=0, concat_axis=0, tiled=True)  17.8 us
    all_to_all x1, blocking collectives, on_device(): fields = lax.all_to_all(sent, AXES, split_axis=0, concat_axis=0, tiled=True)  11.2 us
    pallas_call x7, Pallas kernels, call(): pl.pallas_call(kernel, out_shape=out_shape, in_specs=specs, out_specs=jax...  9.49 us
    ppermute x2, waiting for transfers between devices, on_device(): behind = lax.ppermute(state, AXES, route)  4.08 us
  transfers between devices with their start and end apart: 2, of which 2 were waited for; matrix products, arithmetic and copies ran while one was open for 1% of the time, Pallas kernels for 6%

profile of v2, /device:TPU:1, one launch (start us, length us, event | category | flops | bytes accessed | tf_op | source)
XLA Modules:
  0.0 43.8 jit_solution(16810881362504767261)
XLA Ops:
  0.0 0.0 copy-start
  0.0 0.0 copy-start.1
  0.0 1.5 %shard_map.73.state = f32[64,128]{1,0:T(8,128)S(1)} custom-call(f32[2,128,128]{2,1,0:T(8,128)} %bitcast.5, f32[16,128]{1,0:T(8,128)} %bitcast.7, f32[16,128]{1,0:T(8,128)} %bitcast.8, s32[16,128]{1,0:T(8,128)} %bitcast.9, s32[1,16]{1,0:T(1,128)} %dest_hbm.1), custom_call_target="tpu_custom_call" | custom-call | flops 134217728 | bytes 524288 | tf_op jit(solution)/shard_map/pallas_call | solution.py:380
  1.5 0.1 collective-permute-start
  1.6 0.2 sine_multiply_fusion
  1.8 0.1 fusion.13.rest_3_
  1.9 0.0 copy-start.2
  1.9 0.0 copy-done
  1.9 0.0 copy-done.1
  1.9 0.7 %copy-done.2 = f32[2,32]{1,0:T(2,128)S(1)} copy-done((f32[2,32]{1,0:T(2,128)S(1)}, f32[2,32]{1,0:T(2,128)}, u32[]{:S(2)}) %copy-start.2) | copy-done | bytes 280
  2.5 1.2 %shard_map.74 = (f32[2,128,128]{2,1,0:T(8,128)S(1)}, bf16[256,256]{1,0:T(8,128)(2,1)S(1)}, bf16[256,256]{1,0:T(8,128)(2,1)S(1)}, bf16[64,192]{1,0:T(8,128)(2,1)S(1)}) custom-call(f32[2,128,128]{2,1,0:T(8,128)S(1)} %bitcast.6, f32[64,128]{1,0:T(8,128)S(1)} %shard_map.73.state, f32[2,128,128]{2,1,0:T(8,128)S(1)} %copy-done.1, f32[2,32]{1,0:T(2,128)S(1)} %copy-done.2, ...), custom_call_target="tpu_custom_call" | custom-call | flops 234881024 | bytes 524288 | tf_op jit(solution)/shard_map/pallas_call | solution.py:380
  3.7 2.0 %collective-permute-done.state = f32[64,128]{1,0:T(8,128)S(1)} collective-permute-done((f32[64,128]{1,0:T(8,128)S(1)}, f32[64,128]{1,0:T(8,128)S(1)}, u32[]{:S(2)}, u32[]{:S(2)}) %collective-permute-start) | collective-permute-done | bytes 32800 | tf_op jit(solution)/shard_map/ppermute | solution.py:459
  5.8 1.6 %shard_map.75 = f32[160,2,128]{2,1,0:T(2,128)S(1)} custom-call(f32[2,128,128]{2,1,0:T(8,128)S(1)} %get-tuple-element.12.field, f32[64,128]{1,0:T(8,128)S(1)} %collective-permute-done.state, bf16[256,256]{1,0:T(8,128)(2,1)S(1)} %get-tuple-element.13.high, bf16[256,256]{1,0:T(8,128)(2,1)S(1)} %get-tuple-element.14.low), custom_call_target="tpu_custom_call" | custom-call | flops 369098752 | bytes 524288 | tf_op jit(solution)/shard_map/pallas_call | solution.py:380
  7.3 17.8 %all_to_all.10.data = f32[160,2,128]{2,1,0:T(2,128)S(1)} all-to-all(f32[160,2,128]{2,1,0:T(2,128)S(1)} %shard_map.75), channel_id=1, replica_groups=mesh['cuts'=4,'group'=8] {'cuts','group'}, dimensions={0} | all-to-all | bytes 327680 | tf_op jit(solution)/shard_map/all_to_all | solution.py:484
  25.1 0.3 shard_map.76
  25.4 11.2 %all_to_all.11.fields = f32[96,4,128]{2,1,0:T(4,128)S(1)} all-to-all(f32[96,4,128]{2,1,0:T(4,128)S(1)} %shard_map.76), channel_id=1, replica_groups=mesh['cuts'=4,'group'=8] {'cuts','group'}, dimensions={0} | all-to-all | bytes 393216 | tf_op jit(solution)/shard_map/all_to_all | solution.py:489
  36.6 0.8 %shard_map.77 = (f32[2,128,128]{2,1,0:T(8,128)S(1)}, f32[96,128]{1,0:T(8,128)S(1)}) custom-call(f32[96,4,128]{2,1,0:T(4,128)S(1)} %all_to_all.11.fields), custom_call_target="tpu_custom_call" | custom-call | flops 268435456 | bytes 524288 | tf_op jit(solution)/shard_map/pallas_call | solution.py:380
  37.4 0.1 collective-permute-start.1
  37.5 1.4 %shard_map.78.field = f32[2,128,128]{2,1,0:T(8,128)S(1)} custom-call(f32[2,128,128]{2,1,0:T(8,128)S(1)} %get-tuple-element.15.field, f32[96,128]{1,0:T(8,128)S(1)} %get-tuple-element.16.state, bf16[256,256]{1,0:T(8,128)(2,1)S(1)} %get-tuple-element.13.high, bf16[256,256]{1,0:T(8,128)(2,1)S(1)} %get-tuple-element.14.low), custom_call_target="tpu_custom_call" | custom-call | flops 369098752 | bytes 524288 | tf_op jit(solution)/shard_map/pallas_call | solution.py:380
  38.9 2.1 %collective-permute-done.1.state = f32[96,128]{1,0:T(8,128)S(1)} collective-permute-done((f32[96,128]{1,0:T(8,128)S(1)}, f32[96,128]{1,0:T(8,128)S(1)}, u32[]{:S(2)}, u32[]{:S(2)}) %collective-permute-start.1) | collective-permute-done | bytes 49184 | tf_op jit(solution)/shard_map/ppermute | solution.py:498
  41.0 2.8 %shard_map.79 = f32[2,128,128]{2,1,0:T(8,128)} custom-call(f32[2,128,128]{2,1,0:T(8,128)S(1)} %shard_map.78.field, f32[96,128]{1,0:T(8,128)S(1)} %collective-permute-done.1.state, bf16[256,256]{1,0:T(8,128)(2,1)S(1)} %get-tuple-element.13.high, bf16[256,256]{1,0:T(8,128)(2,1)S(1)} %get-tuple-element.14.low), custom_call_target="tpu_custom_call" | custom-call | flops 637534208 | bytes 524288 | tf_op jit(solution)/shard_map/pallas_call | solution.py:380
  (1 shorter events, 0.0 us)
Async XLA Ops:
  0.0 1.9 %copy-start = (f32[1,2,128,128]{3,2,1,0:T(8,128)S(1)}, f32[1,2,128,128]{3,2,1,0:T(8,128)}, u32[]{:S(2)}) copy-start(f32[1,2,128,128]{3,2,1,0:T(8,128)} %param.7) | copy-start | bytes 393220
  0.0 1.9 %copy-start.1 = (f32[2,128,128]{2,1,0:T(8,128)S(1)}, f32[2,128,128]{2,1,0:T(8,128)}, u32[]{:S(2)}) copy-start(f32[2,128,128]{2,1,0:T(8,128)} %propagator.1) | copy-start | bytes 393220
  1.5 4.3 %collective-permute-start = (f32[64,128]{1,0:T(8,128)S(1)}, f32[64,128]{1,0:T(8,128)S(1)}, u32[]{:S(2)}, u32[]{:S(2)}) collective-permute-start(f32[64,128]{1,0:T(8,128)S(1)} %shard_map.73.state), channel_id=1, source_target_pairs={{1,0},{2,1},{3,2},{4,3},{5,4},{6,5},{7,6},{8,7},{9,8},{10,9},{11,1... | collective-permute-start | bytes 98312 | tf_op jit(solution)/shard_map/ppermute | solution.py:459
  1.9 0.7 %copy-start.2 = (f32[2,32]{1,0:T(2,128)S(1)}, f32[2,32]{1,0:T(2,128)}, u32[]{:S(2)}) copy-start(f32[2,32]{1,0:T(2,128)} %rest_0_.1) | copy-start | bytes 772
  37.4 3.6 %collective-permute-start.1 = (f32[96,128]{1,0:T(8,128)S(1)}, f32[96,128]{1,0:T(8,128)S(1)}, u32[]{:S(2)}, u32[]{:S(2)}) collective-permute-start(f32[96,128]{1,0:T(8,128)S(1)} %get-tuple-element.16.state), channel_id=1, source_target_pairs={{1,0},{2,1},{3,2},{4,3},{5,4},{6,5},{7,6},{8,7},{9,8},{10,9},{11,1... | collective-permute-start | bytes 147464 | tf_op jit(solution)/shard_map/ppermute | solution.py:498

commit v3 on v2

--- a/solution.py
+++ b/solution.py
@@ -100,24 +100,38 @@
     return jnp.where(rows == ids, one, zero)
 
 
-def kick(real, imag, phases, energy, pixels, read_ref, hot_ref=None):
+def kick(real, imag, phases, energy, pixels, read_ref, hot_ref=None, dark=None):
     grid = real.shape[0]
     half = grid // 2
     blocks, size = phases.shape
-    upper, lower = fold(real, imag)
-    low = jnp.concatenate([upper, lower], axis=0).astype(BF16)
     place, col = cells(pixels, grid)
-    for start, width in chunks(blocks):
-        hot = one_hot(place, start, width, 2 * grid)
-        if hot_ref is not None:
-            hot_ref[:, start * size : (start + width) * size] = hot
-        picked = dot(low, hot, 0, 0)
-        col_hit = hits(lanes(col, start, width), half)
-        for part in range(2):
-            value = picked[part * half : (part + 1) * half]
-            value = jnp.sum(jnp.where(col_hit, value, 0.0), axis=0, keepdims=True)
-            for k in range(width):
-                read_ref[part, start + k : start + k + 1, :] = value[:, k * size : (k + 1) * size]
+
+    def read():
+        upper, lower = fold(real, imag)
+        low = jnp.concatenate([upper, lower], axis=0).astype(BF16)
+        for start, width in chunks(blocks):
+            hot = one_hot(place, start, width, 2 * grid)
+            if hot_ref is not None:
+                hot_ref[:, start * size : (start + width) * size] = hot
+            picked = dot(low, hot, 0, 0)
+            col_hit = hits(lanes(col, start, width), half)
+            for part in range(2):
+                value = picked[part * half : (part + 1) * half]
+                value = jnp.sum(jnp.where(col_hit, value, 0.0), axis=0, keepdims=True)
+                for k in range(width):
+                    read_ref[part, start + k : start + k + 1, :] = value[:, k * size : (k + 1) * size]
+
+    if dark is None:
+        read()
+    else:
+        pl.when(jnp.logical_not(dark))(read)
+
+        @pl.when(dark)
+        def _():
+            read_ref[...] = jnp.zeros(read_ref.shape, F32)
+            for start, width in chunks(blocks):
+                hot_ref[:, start * size : (start + width) * size] = one_hot(place, start, width, 2 * grid)
+
     read_real = read_ref[0, :blocks, :]
     read_imag = read_ref[1, :blocks, :]
     energy = energy - KICK_RATE * (read_real * jnp.cos(phases) - read_imag * jnp.sin(phases))
@@ -219,8 +233,16 @@
     radiate(blocks, dropped, field, state, form, out, hot_ref, spread_ref)
 
 
-def radiate_kernel(blocks, dropped, field, state, high, low, out, hot_ref, spread_ref):
-    radiate(blocks, dropped, field, state, (high[...], low[...]), out, hot_ref, spread_ref)
+def third_radiate_kernel(blocks, field, state, high, low, out, hot_ref, spread_ref):
+    needed = position() > 1
+
+    @pl.when(needed)
+    def _():
+        radiate(blocks, 1, field, state, (high[...], low[...]), out, hot_ref, spread_ref)
+
+    @pl.when(jnp.logical_not(needed))
+    def _():
+        out[...] = jnp.zeros(out.shape, F32)
 
 
 def second_kernel(count, rows, cap, field, state, high, low, out, *rest):
@@ -230,7 +252,10 @@
     real, imag = field[0], field[1]
     grid = real.shape[0]
     pixels = state[2 * blocks : 3 * blocks, :].astype(jnp.int32)
-    phases, energy = kick(real, imag, state[0:blocks, :], state[blocks : 2 * blocks, :], pixels, read_ref, hot_ref)
+    dark = position() == count - 1
+    phases, energy = kick(
+        real, imag, state[0:blocks, :], state[blocks : 2 * blocks, :], pixels, read_ref, hot_ref, dark
+    )
     kinds = by_destination((phases, energy, state[2 * blocks : 3 * blocks, :], state[3 * blocks : 4 * blocks, :]))
     if rows:
         pairs, pieces = rows // 2, len(kinds)
@@ -365,14 +390,21 @@
 
 def fourth_kernel(field, state, high, low, out, read_ref, hot_ref, spread_ref):
     blocks = state.shape[0] // 3
-    pixels = state[2 * blocks : 3 * blocks, :].astype(jnp.int32)
-    real, imag = field[0], field[1]
-    phases, _ = kick(real, imag, state[0:blocks, :], state[blocks : 2 * blocks, :], pixels, read_ref, hot_ref)
-    real, imag = emit(real, imag, phases, pixels, hot_ref, spread_ref, True)
-    real, imag = diffract(real, imag, high[...], low[...])
-    keep = kept_unless(0)
-    out[0] = real * keep
-    out[1] = imag * keep
+    needed = position() > 0
+
+    @pl.when(needed)
+    def _():
+        pixels = state[2 * blocks : 3 * blocks, :].astype(jnp.int32)
+        real, imag = field[0], field[1]
+        phases, _ = kick(
+            real, imag, state[0:blocks, :], state[blocks : 2 * blocks, :], pixels, read_ref, hot_ref
+        )
+        real, imag = emit(real, imag, phases, pixels, hot_ref, spread_ref, True)
+        out[0], out[1] = diffract(real, imag, high[...], low[...])
+
+    @pl.when(jnp.logical_not(needed))
+    def _():
+        out[...] = jnp.zeros(out.shape, F32)
 
 
 def call(kernel, out_shape, scratch, flops, args, memory=pltpu.VMEM):
@@ -497,7 +529,7 @@
     )
     behind = lax.ppermute(state, AXES, route)
     field = call(
-        functools.partial(radiate_kernel, capacity, 1), shape(2, grid, grid), hot(capacity),
+        functools.partial(third_radiate_kernel, capacity), shape(2, grid, grid), hot(capacity),
         share * pass_flops + prop_flops, (field, state, *form),
     )
     out = call(

time: 43.9 us -> 43.7 us (level)
  waiting for transfers between devices: 4.08 us -> 5.48 us
  Pallas kernels: 9.49 us -> 8.14 us
    ppermute x2, waiting for transfers between devices: 4.08 us -> 5.48 us  [on_device(): behind = lax.ppermute(state, AXES, route)]
    pallas_call x7, Pallas kernels: 9.49 us -> 8.14 us  [call(): pl.pallas_call(kernel, out_shape=out_shape, in_specs=specs, out_specs=jax...]
  transfers between devices with their start and end apart: 2 -> 2, of which waited for: 2 -> 2; matrix products, arithmetic and copies ran while one was open for 1% -> 1% of each run, Pallas kernels for 6% -> 3%
where the time goes in v3:
time: 43.7 us; the launch traced here: 43.5 us
  blocking collectives  28.7 us (66%)
  Pallas kernels  8.14 us (19%)
  waiting for transfers between devices  5.48 us (13%)
  local copies, waits for them, and re-layouts  0.66 us (2%)
    all_to_all x1, blocking collectives, on_device(): data = lax.all_to_all(field, AXES, split_axis=0, concat_axis=0, tiled=True)  17.5 us
    all_to_all x1, blocking collectives, on_device(): fields = lax.all_to_all(sent, AXES, split_axis=0, concat_axis=0, tiled=True)  11.2 us
    pallas_call x7, Pallas kernels, call(): pl.pallas_call(kernel, out_shape=out_shape, in_specs=specs, out_specs=jax...  8.14 us
    ppermute x2, waiting for transfers between devices, on_device(): behind = lax.ppermute(state, AXES, route)  5.48 us
  transfers between devices with their start and end apart: 2, of which 2 were waited for; matrix products, arithmetic and copies ran while one was open for 1% of the time, Pallas kernels for 3%

profile of v3, /device:TPU:1, one launch (start us, length us, event | category | flops | bytes accessed | tf_op | source)
XLA Modules:
  0.0 43.5 jit_solution(14094696704516083119)
XLA Ops:
  0.0 0.0 copy-start
  0.0 0.0 copy-start.1
  0.0 1.5 %shard_map.73.state = f32[64,128]{1,0:T(8,128)S(1)} custom-call(f32[2,128,128]{2,1,0:T(8,128)} %bitcast.5, f32[16,128]{1,0:T(8,128)} %bitcast.7, f32[16,128]{1,0:T(8,128)} %bitcast.8, s32[16,128]{1,0:T(8,128)} %bitcast.9, s32[1,16]{1,0:T(1,128)} %dest_hbm.1), custom_call_target="tpu_custom_call" | custom-call | flops 134217728 | bytes 524288 | tf_op jit(solution)/shard_map/pallas_call | solution.py:412
  1.5 0.1 collective-permute-start
  1.6 0.2 sine_multiply_fusion
  1.8 0.1 fusion.13.rest_3_
  1.9 0.0 copy-start.2
  1.9 0.0 copy-done
  1.9 0.0 copy-done.1
  1.9 0.7 %copy-done.2 = f32[2,32]{1,0:T(2,128)S(1)} copy-done((f32[2,32]{1,0:T(2,128)S(1)}, f32[2,32]{1,0:T(2,128)}, u32[]{:S(2)}) %copy-start.2) | copy-done | bytes 280
  2.5 1.2 %shard_map.74 = (f32[2,128,128]{2,1,0:T(8,128)S(1)}, bf16[256,256]{1,0:T(8,128)(2,1)S(1)}, bf16[256,256]{1,0:T(8,128)(2,1)S(1)}, bf16[64,192]{1,0:T(8,128)(2,1)S(1)}) custom-call(f32[2,128,128]{2,1,0:T(8,128)S(1)} %bitcast.6, f32[64,128]{1,0:T(8,128)S(1)} %shard_map.73.state, f32[2,128,128]{2,1,0:T(8,128)S(1)} %copy-done.1, f32[2,32]{1,0:T(2,128)S(1)} %copy-done.2, ...), custom_call_target="tpu_custom_call" | custom-call | flops 234881024 | bytes 524288 | tf_op jit(solution)/shard_map/pallas_call | solution.py:412
  3.7 2.0 %collective-permute-done.state = f32[64,128]{1,0:T(8,128)S(1)} collective-permute-done((f32[64,128]{1,0:T(8,128)S(1)}, f32[64,128]{1,0:T(8,128)S(1)}, u32[]{:S(2)}, u32[]{:S(2)}) %collective-permute-start) | collective-permute-done | bytes 32800 | tf_op jit(solution)/shard_map/ppermute | solution.py:491
  5.8 1.6 %shard_map.75 = f32[160,2,128]{2,1,0:T(2,128)S(1)} custom-call(f32[2,128,128]{2,1,0:T(8,128)S(1)} %get-tuple-element.12.field, f32[64,128]{1,0:T(8,128)S(1)} %collective-permute-done.state, bf16[256,256]{1,0:T(8,128)(2,1)S(1)} %get-tuple-element.13.high, bf16[256,256]{1,0:T(8,128)(2,1)S(1)} %get-tuple-element.14.low), custom_call_target="tpu_custom_call" | custom-call | flops 369098752 | bytes 524288 | tf_op jit(solution)/shard_map/pallas_call | solution.py:412
  7.4 17.5 %all_to_all.10.data = f32[160,2,128]{2,1,0:T(2,128)S(1)} all-to-all(f32[160,2,128]{2,1,0:T(2,128)S(1)} %shard_map.75), channel_id=1, replica_groups=mesh['cuts'=4,'group'=8] {'cuts','group'}, dimensions={0} | all-to-all | bytes 327680 | tf_op jit(solution)/shard_map/all_to_all | solution.py:516
  24.9 0.3 shard_map.76
  25.2 11.2 %all_to_all.11.fields = f32[96,4,128]{2,1,0:T(4,128)S(1)} all-to-all(f32[96,4,128]{2,1,0:T(4,128)S(1)} %shard_map.76), channel_id=1, replica_groups=mesh['cuts'=4,'group'=8] {'cuts','group'}, dimensions={0} | all-to-all | bytes 393216 | tf_op jit(solution)/shard_map/all_to_all | solution.py:521
  36.4 0.8 %shard_map.77 = (f32[2,128,128]{2,1,0:T(8,128)S(1)}, f32[96,128]{1,0:T(8,128)S(1)}) custom-call(f32[96,4,128]{2,1,0:T(4,128)S(1)} %all_to_all.11.fields), custom_call_target="tpu_custom_call" | custom-call | flops 268435456 | bytes 524288 | tf_op jit(solution)/shard_map/pallas_call | solution.py:412
  37.2 0.1 collective-permute-start.1
  37.3 3.5 %collective-permute-done.1.state = f32[96,128]{1,0:T(8,128)S(1)} collective-permute-done((f32[96,128]{1,0:T(8,128)S(1)}, f32[96,128]{1,0:T(8,128)S(1)}, u32[]{:S(2)}, u32[]{:S(2)}) %collective-permute-start.1) | collective-permute-done | bytes 49184 | tf_op jit(solution)/shard_map/ppermute | solution.py:530
  40.8 2.8 %shard_map.79 = f32[2,128,128]{2,1,0:T(8,128)} custom-call(f32[2,128,128]{2,1,0:T(8,128)S(1)} %shard_map.78.field, f32[96,128]{1,0:T(8,128)S(1)} %collective-permute-done.1.state, bf16[256,256]{1,0:T(8,128)(2,1)S(1)} %get-tuple-element.13.high, bf16[256,256]{1,0:T(8,128)(2,1)S(1)} %get-tuple-element.14.low), custom_call_target="tpu_custom_call" | custom-call | flops 637534208 | bytes 524288 | tf_op jit(solution)/shard_map/pallas_call | solution.py:412
  (2 shorter events, 0.0 us)
Async XLA Ops:
  0.0 1.9 %copy-start = (f32[1,2,128,128]{3,2,1,0:T(8,128)S(1)}, f32[1,2,128,128]{3,2,1,0:T(8,128)}, u32[]{:S(2)}) copy-start(f32[1,2,128,128]{3,2,1,0:T(8,128)} %param.7) | copy-start | bytes 393220
  0.0 1.9 %copy-start.1 = (f32[2,128,128]{2,1,0:T(8,128)S(1)}, f32[2,128,128]{2,1,0:T(8,128)}, u32[]{:S(2)}) copy-start(f32[2,128,128]{2,1,0:T(8,128)} %propagator.1) | copy-start | bytes 393220
  1.5 4.3 %collective-permute-start = (f32[64,128]{1,0:T(8,128)S(1)}, f32[64,128]{1,0:T(8,128)S(1)}, u32[]{:S(2)}, u32[]{:S(2)}) collective-permute-start(f32[64,128]{1,0:T(8,128)S(1)} %shard_map.73.state), channel_id=1, source_target_pairs={{1,0},{2,1},{3,2},{4,3},{5,4},{6,5},{7,6},{8,7},{9,8},{10,9},{11,1... | collective-permute-start | bytes 98312 | tf_op jit(solution)/shard_map/ppermute | solution.py:491
  1.9 0.7 %copy-start.2 = (f32[2,32]{1,0:T(2,128)S(1)}, f32[2,32]{1,0:T(2,128)}, u32[]{:S(2)}) copy-start(f32[2,32]{1,0:T(2,128)} %rest_0_.1) | copy-start | bytes 772
  37.2 3.6 %collective-permute-start.1 = (f32[96,128]{1,0:T(8,128)S(1)}, f32[96,128]{1,0:T(8,128)S(1)}, u32[]{:S(2)}, u32[]{:S(2)}) collective-permute-start(f32[96,128]{1,0:T(8,128)S(1)} %get-tuple-element.16.state), channel_id=1, source_target_pairs={{1,0},{2,1},{3,2},{4,3},{5,4},{6,5},{7,6},{8,7},{9,8},{10,9},{11,1... | collective-permute-start | bytes 147464 | tf_op jit(solution)/shard_map/ppermute | solution.py:530

commit v4 on v3

--- a/solution.py
+++ b/solution.py
@@ -154,7 +154,7 @@
             value = jnp.where(col_hit, lanes(weight, start, width), 0.0)
             spread_ref[part * half : (part + 1) * half, where] = value.astype(BF16)
     span = blocks * size
-    source = dot(hot_ref[:, :span], spread_ref[:, :span], 1, 1)
+    source = dot(spread_ref[:, :span], hot_ref[:, :span], 1, 1).T
     source_real, source_imag = fold(source[:grid], source[grid:])
     return real + EMIT_RATE * source_real, imag + EMIT_RATE * source_imag
 
@@ -396,8 +396,9 @@
     def _():
         pixels = state[2 * blocks : 3 * blocks, :].astype(jnp.int32)
         real, imag = field[0], field[1]
+        dark = position() == 1
         phases, _ = kick(
-            real, imag, state[0:blocks, :], state[blocks : 2 * blocks, :], pixels, read_ref, hot_ref
+            real, imag, state[0:blocks, :], state[blocks : 2 * blocks, :], pixels, read_ref, hot_ref, dark
         )
         real, imag = emit(real, imag, phases, pixels, hot_ref, spread_ref, True)
         out[0], out[1] = diffract(real, imag, high[...], low[...])

time: 43.7 us -> 43.4 us (level)
  no operation moved by 1% of the time
where the time goes in v4:
time: 43.4 us; the launch traced here: 43.2 us
  blocking collectives  28.7 us (66%)
  Pallas kernels  7.93 us (18%)
  waiting for transfers between devices  5.41 us (12%)
  local copies, waits for them, and re-layouts  0.66 us (2%)
    all_to_all x1, blocking collectives, on_device(): data = lax.all_to_all(field, AXES, split_axis=0, concat_axis=0, tiled=True)  17.5 us
    all_to_all x1, blocking collectives, on_device(): fields = lax.all_to_all(sent, AXES, split_axis=0, concat_axis=0, tiled=True)  11.2 us
    pallas_call x7, Pallas kernels, call(): pl.pallas_call(kernel, out_shape=out_shape, in_specs=specs, out_specs=jax...  7.93 us
    ppermute x2, waiting for transfers between devices, on_device(): behind = lax.ppermute(state, AXES, route)  5.41 us
  transfers between devices with their start and end apart: 2, of which 2 were waited for; matrix products, arithmetic and copies ran while one was open for 1% of the time, Pallas kernels for 3%

profile of v4, /device:TPU:1, one launch (start us, length us, event | category | flops | bytes accessed | tf_op | source)
XLA Modules:
  0.0 43.2 jit_solution(5883173863292813552)
XLA Ops:
  0.0 0.0 copy-start
  0.0 0.0 copy-start.1
  0.0 1.5 %shard_map.73.state = f32[64,128]{1,0:T(8,128)S(1)} custom-call(f32[2,128,128]{2,1,0:T(8,128)} %bitcast.5, f32[16,128]{1,0:T(8,128)} %bitcast.7, f32[16,128]{1,0:T(8,128)} %bitcast.8, s32[16,128]{1,0:T(8,128)} %bitcast.9, s32[1,16]{1,0:T(1,128)} %dest_hbm.1), custom_call_target="tpu_custom_call" | custom-call | flops 134217728 | bytes 524288 | tf_op jit(solution)/shard_map/pallas_call | solution.py:413
  1.5 0.1 collective-permute-start
  1.6 0.2 sine_multiply_fusion
  1.8 0.1 fusion.13.rest_3_
  1.9 0.0 copy-start.2
  1.9 0.0 copy-done
  1.9 0.0 copy-done.1
  1.9 0.7 %copy-done.2 = f32[2,32]{1,0:T(2,128)S(1)} copy-done((f32[2,32]{1,0:T(2,128)S(1)}, f32[2,32]{1,0:T(2,128)}, u32[]{:S(2)}) %copy-start.2) | copy-done | bytes 280
  2.5 1.3 %shard_map.74 = (f32[2,128,128]{2,1,0:T(8,128)S(1)}, bf16[256,256]{1,0:T(8,128)(2,1)S(1)}, bf16[256,256]{1,0:T(8,128)(2,1)S(1)}, bf16[64,192]{1,0:T(8,128)(2,1)S(1)}) custom-call(f32[2,128,128]{2,1,0:T(8,128)S(1)} %bitcast.6, f32[64,128]{1,0:T(8,128)S(1)} %shard_map.73.state, f32[2,128,128]{2,1,0:T(8,128)S(1)} %copy-done.1, f32[2,32]{1,0:T(2,128)S(1)} %copy-done.2, ...), custom_call_target="tpu_custom_call" | custom-call | flops 234881024 | bytes 524288 | tf_op jit(solution)/shard_map/pallas_call | solution.py:413
  3.8 1.9 %collective-permute-done.state = f32[64,128]{1,0:T(8,128)S(1)} collective-permute-done((f32[64,128]{1,0:T(8,128)S(1)}, f32[64,128]{1,0:T(8,128)S(1)}, u32[]{:S(2)}, u32[]{:S(2)}) %collective-permute-start) | collective-permute-done | bytes 32800 | tf_op jit(solution)/shard_map/ppermute | solution.py:492
  5.8 1.6 %shard_map.75 = f32[160,2,128]{2,1,0:T(2,128)S(1)} custom-call(f32[2,128,128]{2,1,0:T(8,128)S(1)} %get-tuple-element.12.field, f32[64,128]{1,0:T(8,128)S(1)} %collective-permute-done.state, bf16[256,256]{1,0:T(8,128)(2,1)S(1)} %get-tuple-element.13.high, bf16[256,256]{1,0:T(8,128)(2,1)S(1)} %get-tuple-element.14.low), custom_call_target="tpu_custom_call" | custom-call | flops 369098752 | bytes 524288 | tf_op jit(solution)/shard_map/pallas_call | solution.py:413
  7.4 17.5 %all_to_all.10.data = f32[160,2,128]{2,1,0:T(2,128)S(1)} all-to-all(f32[160,2,128]{2,1,0:T(2,128)S(1)} %shard_map.75), channel_id=1, replica_groups=mesh['cuts'=4,'group'=8] {'cuts','group'}, dimensions={0} | all-to-all | bytes 327680 | tf_op jit(solution)/shard_map/all_to_all | solution.py:517
  24.9 0.3 shard_map.76
  25.2 11.2 %all_to_all.11.fields = f32[96,4,128]{2,1,0:T(4,128)S(1)} all-to-all(f32[96,4,128]{2,1,0:T(4,128)S(1)} %shard_map.76), channel_id=1, replica_groups=mesh['cuts'=4,'group'=8] {'cuts','group'}, dimensions={0} | all-to-all | bytes 393216 | tf_op jit(solution)/shard_map/all_to_all | solution.py:522
  36.4 0.8 %shard_map.77 = (f32[2,128,128]{2,1,0:T(8,128)S(1)}, f32[96,128]{1,0:T(8,128)S(1)}) custom-call(f32[96,4,128]{2,1,0:T(4,128)S(1)} %all_to_all.11.fields), custom_call_target="tpu_custom_call" | custom-call | flops 268435456 | bytes 524288 | tf_op jit(solution)/shard_map/pallas_call | solution.py:413
  37.2 0.1 collective-permute-start.1
  37.3 3.5 %collective-permute-done.1.state = f32[96,128]{1,0:T(8,128)S(1)} collective-permute-done((f32[96,128]{1,0:T(8,128)S(1)}, f32[96,128]{1,0:T(8,128)S(1)}, u32[]{:S(2)}, u32[]{:S(2)}) %collective-permute-start.1) | collective-permute-done | bytes 49184 | tf_op jit(solution)/shard_map/ppermute | solution.py:531
  40.8 2.5 %shard_map.79 = f32[2,128,128]{2,1,0:T(8,128)} custom-call(f32[2,128,128]{2,1,0:T(8,128)S(1)} %shard_map.78.field, f32[96,128]{1,0:T(8,128)S(1)} %collective-permute-done.1.state, bf16[256,256]{1,0:T(8,128)(2,1)S(1)} %get-tuple-element.13.high, bf16[256,256]{1,0:T(8,128)(2,1)S(1)} %get-tuple-element.14.low), custom_call_target="tpu_custom_call" | custom-call | flops 637534208 | bytes 524288 | tf_op jit(solution)/shard_map/pallas_call | solution.py:413
  (2 shorter events, 0.0 us)
Async XLA Ops:
  0.0 1.9 %copy-start = (f32[1,2,128,128]{3,2,1,0:T(8,128)S(1)}, f32[1,2,128,128]{3,2,1,0:T(8,128)}, u32[]{:S(2)}) copy-start(f32[1,2,128,128]{3,2,1,0:T(8,128)} %param.7) | copy-start | bytes 393220
  0.0 1.9 %copy-start.1 = (f32[2,128,128]{2,1,0:T(8,128)S(1)}, f32[2,128,128]{2,1,0:T(8,128)}, u32[]{:S(2)}) copy-start(f32[2,128,128]{2,1,0:T(8,128)} %propagator.1) | copy-start | bytes 393220
  1.5 4.3 %collective-permute-start = (f32[64,128]{1,0:T(8,128)S(1)}, f32[64,128]{1,0:T(8,128)S(1)}, u32[]{:S(2)}, u32[]{:S(2)}) collective-permute-start(f32[64,128]{1,0:T(8,128)S(1)} %shard_map.73.state), channel_id=1, source_target_pairs={{1,0},{2,1},{3,2},{4,3},{5,4},{6,5},{7,6},{8,7},{9,8},{10,9},{11,1... | collective-permute-start | bytes 98312 | tf_op jit(solution)/shard_map/ppermute | solution.py:492
  1.9 0.7 %copy-start.2 = (f32[2,32]{1,0:T(2,128)S(1)}, f32[2,32]{1,0:T(2,128)}, u32[]{:S(2)}) copy-start(f32[2,32]{1,0:T(2,128)} %rest_0_.1) | copy-start | bytes 772
  37.2 3.6 %collective-permute-start.1 = (f32[96,128]{1,0:T(8,128)S(1)}, f32[96,128]{1,0:T(8,128)S(1)}, u32[]{:S(2)}, u32[]{:S(2)}) collective-permute-start(f32[96,128]{1,0:T(8,128)S(1)} %get-tuple-element.16.state), channel_id=1, source_target_pairs={{1,0},{2,1},{3,2},{4,3},{5,4},{6,5},{7,6},{8,7},{9,8},{10,9},{11,1... | collective-permute-start | bytes 147464 | tf_op jit(solution)/shard_map/ppermute | solution.py:531

commit v5 on v4

--- a/solution.py
+++ b/solution.py
@@ -100,7 +100,12 @@
     return jnp.where(rows == ids, one, zero)
 
 
-def kick(real, imag, phases, energy, pixels, read_ref, hot_ref=None, dark=None):
+def fill(place, blocks, size, span, hot_ref):
+    for start, width in chunks(blocks):
+        hot_ref[:, start * size : (start + width) * size] = one_hot(place, start, width, span)
+
+
+def kick(real, imag, phases, energy, pixels, read_ref, hot_ref=None, dark=None, turn=None):
     grid = real.shape[0]
     half = grid // 2
     blocks, size = phases.shape
@@ -110,9 +115,10 @@
         upper, lower = fold(real, imag)
         low = jnp.concatenate([upper, lower], axis=0).astype(BF16)
         for start, width in chunks(blocks):
-            hot = one_hot(place, start, width, 2 * grid)
-            if hot_ref is not None:
-                hot_ref[:, start * size : (start + width) * size] = hot
+            where = slice(start * size, (start + width) * size)
+            hot = hot_ref[:, where] if turn else one_hot(place, start, width, 2 * grid)
+            if hot_ref is not None and not turn:
+                hot_ref[:, where] = hot
             picked = dot(low, hot, 0, 0)
             col_hit = hits(lanes(col, start, width), half)
             for part in range(2):
@@ -129,12 +135,12 @@
         @pl.when(dark)
         def _():
             read_ref[...] = jnp.zeros(read_ref.shape, F32)
-            for start, width in chunks(blocks):
-                hot_ref[:, start * size : (start + width) * size] = one_hot(place, start, width, 2 * grid)
-
+            fill(place, blocks, size, 2 * grid, hot_ref)
+
+    cosine, sine = turn or (jnp.cos(phases), jnp.sin(phases))
     read_real = read_ref[0, :blocks, :]
     read_imag = read_ref[1, :blocks, :]
-    energy = energy - KICK_RATE * (read_real * jnp.cos(phases) - read_imag * jnp.sin(phases))
+    energy = energy - KICK_RATE * (read_real * cosine - read_imag * sine)
     return phases + PHASE_RATE * energy, energy
 
 
@@ -154,7 +160,7 @@
             value = jnp.where(col_hit, lanes(weight, start, width), 0.0)
             spread_ref[part * half : (part + 1) * half, where] = value.astype(BF16)
     span = blocks * size
-    source = dot(spread_ref[:, :span], hot_ref[:, :span], 1, 1).T
+    source = dot(hot_ref[:, :span], spread_ref[:, :span], 1, 1)
     source_real, source_imag = fold(source[:grid], source[grid:])
     return real + EMIT_RATE * source_real, imag + EMIT_RATE * source_imag
 
@@ -167,22 +173,29 @@
     return jnp.where(position() == index, 0.0, 1.0).astype(F32)
 
 
-def kick_kernel(field_hbm, phases_hbm, energy_hbm, pixels_hbm, dest_hbm, out, field, phases, energy, pixels, dest, read_ref, sems):
+def kick_kernel(field_hbm, phases_hbm, energy_hbm, pixels_hbm, dest_hbm, out, field, phases, energy, pixels, dest, read_ref, hot_ref, sems):
     blocks, size = phases.shape
-    pairs = ((field_hbm, field), (pixels_hbm, pixels), (phases_hbm, phases), (energy_hbm, energy), (dest_hbm, dest))
+    pairs = ((pixels_hbm, pixels), (phases_hbm, phases), (energy_hbm, energy), (dest_hbm, dest), (field_hbm, field))
     copies = [pltpu.make_async_copy(source, target, sems.at[k]) for k, (source, target) in enumerate(pairs)]
     for copy in copies:
         copy.start()
-    for copy in copies:
+    for copy in copies[:-1]:
         copy.wait()
-    new_phases, new_energy = kick(field[0], field[1], phases[...], energy[...], pixels[...], read_ref)
-    out[0:blocks, :] = new_phases
-    out[blocks : 2 * blocks, :] = new_energy
-    out[2 * blocks : 3 * blocks, :] = pixels[...].astype(F32)
+    grid = field.shape[1]
+    place, _ = cells(pixels[...], grid)
+    fill(place, blocks, size, 2 * grid, hot_ref)
+    turn = (jnp.cos(phases[...]), jnp.sin(phases[...]))
     square = (blocks, blocks)
     own = lax.broadcasted_iota(jnp.int32, square, 0) == lax.broadcasted_iota(jnp.int32, square, 1)
     goals = jnp.where(own, jnp.broadcast_to(dest[0:1, :].astype(F32), square), 0.0)
     out[3 * blocks : 4 * blocks, :] = jnp.broadcast_to(jnp.sum(goals, axis=1, keepdims=True), (blocks, size))
+    out[2 * blocks : 3 * blocks, :] = pixels[...].astype(F32)
+    copies[-1].wait()
+    new_phases, new_energy = kick(
+        field[0], field[1], phases[...], energy[...], pixels[...], read_ref, hot_ref, turn=turn
+    )
+    out[0:blocks, :] = new_phases
+    out[blocks : 2 * blocks, :] = new_energy
 
 
 def by_destination(kinds):
@@ -484,6 +497,7 @@
             pltpu.VMEM((blocks, size), jnp.int32),
             pltpu.VMEM((1, blocks), jnp.int32),
             read(blocks),
+            hot(blocks)[0],
             pltpu.SemaphoreType.DMA((5,)),
         ],
         pass_flops, tuple(pltpu.with_memory_space_constraint(value, pltpu.HBM) for value in given), pl.ANY,

time: 43.4 us -> 43.4 us (level)
  no operation moved by 1% of the time
where the time goes in v5:
time: 43.4 us; the launch traced here: 43.2 us
  blocking collectives  28.7 us (66%)
  Pallas kernels  7.83 us (18%)
  waiting for transfers between devices  5.47 us (13%)
  local copies, waits for them, and re-layouts  0.66 us (2%)
    all_to_all x1, blocking collectives, on_device(): data = lax.all_to_all(field, AXES, split_axis=0, concat_axis=0, tiled=True)  17.5 us
    all_to_all x1, blocking collectives, on_device(): fields = lax.all_to_all(sent, AXES, split_axis=0, concat_axis=0, tiled=True)  11.2 us
    pallas_call x7, Pallas kernels, call(): pl.pallas_call(kernel, out_shape=out_shape, in_specs=specs, out_specs=jax...  7.83 us
    ppermute x2, waiting for transfers between devices, on_device(): behind = lax.ppermute(state, AXES, route)  5.47 us
  transfers between devices with their start and end apart: 2, of which 2 were waited for; matrix products, arithmetic and copies ran while one was open for 1% of the time, Pallas kernels for 3%

profile of v5, /device:TPU:1, one launch (start us, length us, event | category | flops | bytes accessed | tf_op | source)
XLA Modules:
  0.0 43.2 jit_solution(9261873381641137662)
XLA Ops:
  0.0 0.0 copy-start
  0.0 0.0 copy-start.1
  0.0 1.5 %shard_map.73.state = f32[64,128]{1,0:T(8,128)S(1)} custom-call(f32[2,128,128]{2,1,0:T(8,128)} %bitcast.5, f32[16,128]{1,0:T(8,128)} %bitcast.7, f32[16,128]{1,0:T(8,128)} %bitcast.8, s32[16,128]{1,0:T(8,128)} %bitcast.9, s32[1,16]{1,0:T(1,128)} %dest_hbm.1), custom_call_target="tpu_custom_call" | custom-call | flops 134217728 | bytes 524288 | tf_op jit(solution)/shard_map/pallas_call | solution.py:426
  1.5 0.1 collective-permute-start
  1.6 0.2 sine_multiply_fusion
  1.8 0.1 fusion.13.rest_3_
  1.9 0.0 copy-start.2
  1.9 0.0 copy-done
  1.9 0.0 copy-done.1
  1.9 0.7 %copy-done.2 = f32[2,32]{1,0:T(2,128)S(1)} copy-done((f32[2,32]{1,0:T(2,128)S(1)}, f32[2,32]{1,0:T(2,128)}, u32[]{:S(2)}) %copy-start.2) | copy-done | bytes 280
  2.6 1.2 %shard_map.74 = (f32[2,128,128]{2,1,0:T(8,128)S(1)}, bf16[256,256]{1,0:T(8,128)(2,1)S(1)}, bf16[256,256]{1,0:T(8,128)(2,1)S(1)}, bf16[64,192]{1,0:T(8,128)(2,1)S(1)}) custom-call(f32[2,128,128]{2,1,0:T(8,128)S(1)} %bitcast.6, f32[64,128]{1,0:T(8,128)S(1)} %shard_map.73.state, f32[2,128,128]{2,1,0:T(8,128)S(1)} %copy-done.1, f32[2,32]{1,0:T(2,128)S(1)} %copy-done.2, ...), custom_call_target="tpu_custom_call" | custom-call | flops 234881024 | bytes 524288 | tf_op jit(solution)/shard_map/pallas_call | solution.py:426
  3.8 2.0 %collective-permute-done.state = f32[64,128]{1,0:T(8,128)S(1)} collective-permute-done((f32[64,128]{1,0:T(8,128)S(1)}, f32[64,128]{1,0:T(8,128)S(1)}, u32[]{:S(2)}, u32[]{:S(2)}) %collective-permute-start) | collective-permute-done | bytes 32800 | tf_op jit(solution)/shard_map/ppermute | solution.py:506
  5.8 1.6 %shard_map.75 = f32[160,2,128]{2,1,0:T(2,128)S(1)} custom-call(f32[2,128,128]{2,1,0:T(8,128)S(1)} %get-tuple-element.12.field, f32[64,128]{1,0:T(8,128)S(1)} %collective-permute-done.state, bf16[256,256]{1,0:T(8,128)(2,1)S(1)} %get-tuple-element.13.high, bf16[256,256]{1,0:T(8,128)(2,1)S(1)} %get-tuple-element.14.low), custom_call_target="tpu_custom_call" | custom-call | flops 369098752 | bytes 524288 | tf_op jit(solution)/shard_map/pallas_call | solution.py:426
  7.4 17.5 %all_to_all.10.data = f32[160,2,128]{2,1,0:T(2,128)S(1)} all-to-all(f32[160,2,128]{2,1,0:T(2,128)S(1)} %shard_map.75), channel_id=1, replica_groups=mesh['cuts'=4,'group'=8] {'cuts','group'}, dimensions={0} | all-to-all | bytes 327680 | tf_op jit(solution)/shard_map/all_to_all | solution.py:531
  24.9 0.3 shard_map.76
  25.2 11.2 %all_to_all.11.fields = f32[96,4,128]{2,1,0:T(4,128)S(1)} all-to-all(f32[96,4,128]{2,1,0:T(4,128)S(1)} %shard_map.76), channel_id=1, replica_groups=mesh['cuts'=4,'group'=8] {'cuts','group'}, dimensions={0} | all-to-all | bytes 393216 | tf_op jit(solution)/shard_map/all_to_all | solution.py:536
  36.4 0.8 %shard_map.77 = (f32[2,128,128]{2,1,0:T(8,128)S(1)}, f32[96,128]{1,0:T(8,128)S(1)}) custom-call(f32[96,4,128]{2,1,0:T(4,128)S(1)} %all_to_all.11.fields), custom_call_target="tpu_custom_call" | custom-call | flops 268435456 | bytes 524288 | tf_op jit(solution)/shard_map/pallas_call | solution.py:426
  37.2 0.1 collective-permute-start.1
  37.3 3.5 %collective-permute-done.1.state = f32[96,128]{1,0:T(8,128)S(1)} collective-permute-done((f32[96,128]{1,0:T(8,128)S(1)}, f32[96,128]{1,0:T(8,128)S(1)}, u32[]{:S(2)}, u32[]{:S(2)}) %collective-permute-start.1) | collective-permute-done | bytes 49184 | tf_op jit(solution)/shard_map/ppermute | solution.py:545
  40.8 2.4 %shard_map.79 = f32[2,128,128]{2,1,0:T(8,128)} custom-call(f32[2,128,128]{2,1,0:T(8,128)S(1)} %shard_map.78.field, f32[96,128]{1,0:T(8,128)S(1)} %collective-permute-done.1.state, bf16[256,256]{1,0:T(8,128)(2,1)S(1)} %get-tuple-element.13.high, bf16[256,256]{1,0:T(8,128)(2,1)S(1)} %get-tuple-element.14.low), custom_call_target="tpu_custom_call" | custom-call | flops 637534208 | bytes 524288 | tf_op jit(solution)/shard_map/pallas_call | solution.py:426
  (2 shorter events, 0.0 us)
Async XLA Ops:
  0.0 1.9 %copy-start = (f32[1,2,128,128]{3,2,1,0:T(8,128)S(1)}, f32[1,2,128,128]{3,2,1,0:T(8,128)}, u32[]{:S(2)}) copy-start(f32[1,2,128,128]{3,2,1,0:T(8,128)} %param.7) | copy-start | bytes 393220
  0.0 1.9 %copy-start.1 = (f32[2,128,128]{2,1,0:T(8,128)S(1)}, f32[2,128,128]{2,1,0:T(8,128)}, u32[]{:S(2)}) copy-start(f32[2,128,128]{2,1,0:T(8,128)} %propagator.1) | copy-start | bytes 393220
  1.5 4.3 %collective-permute-start = (f32[64,128]{1,0:T(8,128)S(1)}, f32[64,128]{1,0:T(8,128)S(1)}, u32[]{:S(2)}, u32[]{:S(2)}) collective-permute-start(f32[64,128]{1,0:T(8,128)S(1)} %shard_map.73.state), channel_id=1, source_target_pairs={{1,0},{2,1},{3,2},{4,3},{5,4},{6,5},{7,6},{8,7},{9,8},{10,9},{11,1... | collective-permute-start | bytes 98312 | tf_op jit(solution)/shard_map/ppermute | solution.py:506
  1.9 0.7 %copy-start.2 = (f32[2,32]{1,0:T(2,128)S(1)}, f32[2,32]{1,0:T(2,128)}, u32[]{:S(2)}) copy-start(f32[2,32]{1,0:T(2,128)} %rest_0_.1) | copy-start | bytes 772
  37.2 3.6 %collective-permute-start.1 = (f32[96,128]{1,0:T(8,128)S(1)}, f32[96,128]{1,0:T(8,128)S(1)}, u32[]{:S(2)}, u32[]{:S(2)}) collective-permute-start(f32[96,128]{1,0:T(8,128)S(1)} %get-tuple-element.16.state), channel_id=1, source_target_pairs={{1,0},{2,1},{3,2},{4,3},{5,4},{6,5},{7,6},{8,7},{9,8},{10,9},{11,1... | collective-permute-start | bytes 147464 | tf_op jit(solution)/shard_map/ppermute | solution.py:545

commit v6 on v5

--- a/solution.py
+++ b/solution.py
@@ -79,7 +79,7 @@
 
 
 def chunks(blocks):
-    width = 2 if blocks % 2 == 0 else 1
+    width = next(width for width in (4, 2, 1) if blocks % width == 0)
     return [(start, width) for start in range(0, blocks, width)]
 
 

time: 43.4 us -> 43.3 us (level)
  no operation moved by 1% of the time
where the time goes in v6:
time: 43.3 us; the launch traced here: 43.1 us
  blocking collectives  28.7 us (66%)
  Pallas kernels  7.77 us (18%)
  waiting for transfers between devices  5.48 us (13%)
  local copies, waits for them, and re-layouts  0.66 us (2%)
    all_to_all x1, blocking collectives, on_device(): data = lax.all_to_all(field, AXES, split_axis=0, concat_axis=0, tiled=True)  17.5 us
    all_to_all x1, blocking collectives, on_device(): fields = lax.all_to_all(sent, AXES, split_axis=0, concat_axis=0, tiled=True)  11.2 us
    pallas_call x7, Pallas kernels, call(): pl.pallas_call(kernel, out_shape=out_shape, in_specs=specs, out_specs=jax...  7.77 us
    ppermute x2, waiting for transfers between devices, on_device(): behind = lax.ppermute(state, AXES, route)  5.48 us
  transfers between devices with their start and end apart: 2, of which 2 were waited for; matrix products, arithmetic and copies ran while one was open for 1% of the time, Pallas kernels for 3%

profile of v6, /device:TPU:1, one launch (start us, length us, event | category | flops | bytes accessed | tf_op | source)
XLA Modules:
  0.0 43.1 jit_solution(13372501614358905719)
XLA Ops:
  0.0 0.0 copy-start
  0.0 0.0 copy-start.1
  0.0 1.5 %shard_map.73.state = f32[64,128]{1,0:T(8,128)S(1)} custom-call(f32[2,128,128]{2,1,0:T(8,128)} %bitcast.5, f32[16,128]{1,0:T(8,128)} %bitcast.7, f32[16,128]{1,0:T(8,128)} %bitcast.8, s32[16,128]{1,0:T(8,128)} %bitcast.9, s32[1,16]{1,0:T(1,128)} %dest_hbm.1), custom_call_target="tpu_custom_call" | custom-call | flops 134217728 | bytes 524288 | tf_op jit(solution)/shard_map/pallas_call | solution.py:426
  1.5 0.1 collective-permute-start
  1.6 0.2 sine_multiply_fusion
  1.8 0.1 fusion.13.rest_3_
  1.9 0.0 copy-start.2
  1.9 0.0 copy-done
  1.9 0.0 copy-done.1
  1.9 0.7 %copy-done.2 = f32[2,32]{1,0:T(2,128)S(1)} copy-done((f32[2,32]{1,0:T(2,128)S(1)}, f32[2,32]{1,0:T(2,128)}, u32[]{:S(2)}) %copy-start.2) | copy-done | bytes 280
  2.6 1.2 %shard_map.74 = (f32[2,128,128]{2,1,0:T(8,128)S(1)}, bf16[256,256]{1,0:T(8,128)(2,1)S(1)}, bf16[256,256]{1,0:T(8,128)(2,1)S(1)}, bf16[64,192]{1,0:T(8,128)(2,1)S(1)}) custom-call(f32[2,128,128]{2,1,0:T(8,128)S(1)} %bitcast.6, f32[64,128]{1,0:T(8,128)S(1)} %shard_map.73.state, f32[2,128,128]{2,1,0:T(8,128)S(1)} %copy-done.1, f32[2,32]{1,0:T(2,128)S(1)} %copy-done.2, ...), custom_call_target="tpu_custom_call" | custom-call | flops 234881024 | bytes 524288 | tf_op jit(solution)/shard_map/pallas_call | solution.py:426
  3.7 2.0 %collective-permute-done.state = f32[64,128]{1,0:T(8,128)S(1)} collective-permute-done((f32[64,128]{1,0:T(8,128)S(1)}, f32[64,128]{1,0:T(8,128)S(1)}, u32[]{:S(2)}, u32[]{:S(2)}) %collective-permute-start) | collective-permute-done | bytes 32800 | tf_op jit(solution)/shard_map/ppermute | solution.py:506
  5.8 1.6 %shard_map.75 = f32[160,2,128]{2,1,0:T(2,128)S(1)} custom-call(f32[2,128,128]{2,1,0:T(8,128)S(1)} %get-tuple-element.12.field, f32[64,128]{1,0:T(8,128)S(1)} %collective-permute-done.state, bf16[256,256]{1,0:T(8,128)(2,1)S(1)} %get-tuple-element.13.high, bf16[256,256]{1,0:T(8,128)(2,1)S(1)} %get-tuple-element.14.low), custom_call_target="tpu_custom_call" | custom-call | flops 369098752 | bytes 524288 | tf_op jit(solution)/shard_map/pallas_call | solution.py:426
  7.4 17.5 %all_to_all.10.data = f32[160,2,128]{2,1,0:T(2,128)S(1)} all-to-all(f32[160,2,128]{2,1,0:T(2,128)S(1)} %shard_map.75), channel_id=1, replica_groups=mesh['cuts'=4,'group'=8] {'cuts','group'}, dimensions={0} | all-to-all | bytes 327680 | tf_op jit(solution)/shard_map/all_to_all | solution.py:531
  24.9 0.3 shard_map.76
  25.2 11.2 %all_to_all.11.fields = f32[96,4,128]{2,1,0:T(4,128)S(1)} all-to-all(f32[96,4,128]{2,1,0:T(4,128)S(1)} %shard_map.76), channel_id=1, replica_groups=mesh['cuts'=4,'group'=8] {'cuts','group'}, dimensions={0} | all-to-all | bytes 393216 | tf_op jit(solution)/shard_map/all_to_all | solution.py:536
  36.4 0.8 %shard_map.77 = (f32[2,128,128]{2,1,0:T(8,128)S(1)}, f32[96,128]{1,0:T(8,128)S(1)}) custom-call(f32[96,4,128]{2,1,0:T(4,128)S(1)} %all_to_all.11.fields), custom_call_target="tpu_custom_call" | custom-call | flops 268435456 | bytes 524288 | tf_op jit(solution)/shard_map/pallas_call | solution.py:426
  37.2 0.1 collective-permute-start.1
  37.3 3.5 %collective-permute-done.1.state = f32[96,128]{1,0:T(8,128)S(1)} collective-permute-done((f32[96,128]{1,0:T(8,128)S(1)}, f32[96,128]{1,0:T(8,128)S(1)}, u32[]{:S(2)}, u32[]{:S(2)}) %collective-permute-start.1) | collective-permute-done | bytes 49184 | tf_op jit(solution)/shard_map/ppermute | solution.py:545
  40.8 2.4 %shard_map.79 = f32[2,128,128]{2,1,0:T(8,128)} custom-call(f32[2,128,128]{2,1,0:T(8,128)S(1)} %shard_map.78.field, f32[96,128]{1,0:T(8,128)S(1)} %collective-permute-done.1.state, bf16[256,256]{1,0:T(8,128)(2,1)S(1)} %get-tuple-element.13.high, bf16[256,256]{1,0:T(8,128)(2,1)S(1)} %get-tuple-element.14.low), custom_call_target="tpu_custom_call" | custom-call | flops 637534208 | bytes 524288 | tf_op jit(solution)/shard_map/pallas_call | solution.py:426
  (2 shorter events, 0.0 us)
Async XLA Ops:
  0.0 1.9 %copy-start = (f32[1,2,128,128]{3,2,1,0:T(8,128)S(1)}, f32[1,2,128,128]{3,2,1,0:T(8,128)}, u32[]{:S(2)}) copy-start(f32[1,2,128,128]{3,2,1,0:T(8,128)} %param.7) | copy-start | bytes 393220
  0.0 1.9 %copy-start.1 = (f32[2,128,128]{2,1,0:T(8,128)S(1)}, f32[2,128,128]{2,1,0:T(8,128)}, u32[]{:S(2)}) copy-start(f32[2,128,128]{2,1,0:T(8,128)} %propagator.1) | copy-start | bytes 393220
  1.5 4.3 %collective-permute-start = (f32[64,128]{1,0:T(8,128)S(1)}, f32[64,128]{1,0:T(8,128)S(1)}, u32[]{:S(2)}, u32[]{:S(2)}) collective-permute-start(f32[64,128]{1,0:T(8,128)S(1)} %shard_map.73.state), channel_id=1, source_target_pairs={{1,0},{2,1},{3,2},{4,3},{5,4},{6,5},{7,6},{8,7},{9,8},{10,9},{11,1... | collective-permute-start | bytes 98312 | tf_op jit(solution)/shard_map/ppermute | solution.py:506
  1.9 0.7 %copy-start.2 = (f32[2,32]{1,0:T(2,128)S(1)}, f32[2,32]{1,0:T(2,128)}, u32[]{:S(2)}) copy-start(f32[2,32]{1,0:T(2,128)} %rest_0_.1) | copy-start | bytes 772
  37.2 3.6 %collective-permute-start.1 = (f32[96,128]{1,0:T(8,128)S(1)}, f32[96,128]{1,0:T(8,128)S(1)}, u32[]{:S(2)}, u32[]{:S(2)}) collective-permute-start(f32[96,128]{1,0:T(8,128)S(1)} %get-tuple-element.16.state), channel_id=1, source_target_pairs={{1,0},{2,1},{3,2},{4,3},{5,4},{6,5},{7,6},{8,7},{9,8},{10,9},{11,1... | collective-permute-start | bytes 147464 | tf_op jit(solution)/shard_map/ppermute | solution.py:545

commit v7 on v6

--- a/solution.py
+++ b/solution.py
@@ -79,7 +79,7 @@
 
 
 def chunks(blocks):
-    width = next(width for width in (4, 2, 1) if blocks % width == 0)
+    width = next(width for width in (8, 4, 2, 1) if blocks % width == 0)
     return [(start, width) for start in range(0, blocks, width)]
 
 

time: 43.3 us -> 43.3 us (level)
  no operation moved by 1% of the time
where the time goes in v7:
time: 43.3 us; the launch traced here: 43.2 us
  blocking collectives  28.7 us (66%)
  Pallas kernels  7.82 us (18%)
  waiting for transfers between devices  5.47 us (13%)
  local copies, waits for them, and re-layouts  0.66 us (2%)
    all_to_all x1, blocking collectives, on_device(): data = lax.all_to_all(field, AXES, split_axis=0, concat_axis=0, tiled=True)  17.5 us
    all_to_all x1, blocking collectives, on_device(): fields = lax.all_to_all(sent, AXES, split_axis=0, concat_axis=0, tiled=True)  11.2 us
    pallas_call x7, Pallas kernels, call(): pl.pallas_call(kernel, out_shape=out_shape, in_specs=specs, out_specs=jax...  7.82 us
    ppermute x2, waiting for transfers between devices, on_device(): behind = lax.ppermute(state, AXES, route)  5.47 us
  transfers between devices with their start and end apart: 2, of which 2 were waited for; matrix products, arithmetic and copies ran while one was open for 1% of the time, Pallas kernels for 3%

profile of v7, /device:TPU:1, one launch (start us, length us, event | category | flops | bytes accessed | tf_op | source)
XLA Modules:
  0.0 43.2 jit_solution(4573331502705117415)
XLA Ops:
  0.0 0.0 copy-start
  0.0 0.0 copy-start.1
  0.0 1.5 %shard_map.73.state = f32[64,128]{1,0:T(8,128)S(1)} custom-call(f32[2,128,128]{2,1,0:T(8,128)} %bitcast.5, f32[16,128]{1,0:T(8,128)} %bitcast.7, f32[16,128]{1,0:T(8,128)} %bitcast.8, s32[16,128]{1,0:T(8,128)} %bitcast.9, s32[1,16]{1,0:T(1,128)} %dest_hbm.1), custom_call_target="tpu_custom_call" | custom-call | flops 134217728 | bytes 524288 | tf_op jit(solution)/shard_map/pallas_call | solution.py:426
  1.5 0.1 collective-permute-start
  1.6 0.2 sine_multiply_fusion
  1.8 0.1 fusion.13.rest_3_
  1.9 0.0 copy-start.2
  1.9 0.0 copy-done
  1.9 0.0 copy-done.1
  1.9 0.7 %copy-done.2 = f32[2,32]{1,0:T(2,128)S(1)} copy-done((f32[2,32]{1,0:T(2,128)S(1)}, f32[2,32]{1,0:T(2,128)}, u32[]{:S(2)}) %copy-start.2) | copy-done | bytes 280
  2.6 1.2 %shard_map.74 = (f32[2,128,128]{2,1,0:T(8,128)S(1)}, bf16[256,256]{1,0:T(8,128)(2,1)S(1)}, bf16[256,256]{1,0:T(8,128)(2,1)S(1)}, bf16[64,192]{1,0:T(8,128)(2,1)S(1)}) custom-call(f32[2,128,128]{2,1,0:T(8,128)S(1)} %bitcast.6, f32[64,128]{1,0:T(8,128)S(1)} %shard_map.73.state, f32[2,128,128]{2,1,0:T(8,128)S(1)} %copy-done.1, f32[2,32]{1,0:T(2,128)S(1)} %copy-done.2, ...), custom_call_target="tpu_custom_call" | custom-call | flops 234881024 | bytes 524288 | tf_op jit(solution)/shard_map/pallas_call | solution.py:426
  3.8 2.0 %collective-permute-done.state = f32[64,128]{1,0:T(8,128)S(1)} collective-permute-done((f32[64,128]{1,0:T(8,128)S(1)}, f32[64,128]{1,0:T(8,128)S(1)}, u32[]{:S(2)}, u32[]{:S(2)}) %collective-permute-start) | collective-permute-done | bytes 32800 | tf_op jit(solution)/shard_map/ppermute | solution.py:506
  5.8 1.6 %shard_map.75 = f32[160,2,128]{2,1,0:T(2,128)S(1)} custom-call(f32[2,128,128]{2,1,0:T(8,128)S(1)} %get-tuple-element.12.field, f32[64,128]{1,0:T(8,128)S(1)} %collective-permute-done.state, bf16[256,256]{1,0:T(8,128)(2,1)S(1)} %get-tuple-element.13.high, bf16[256,256]{1,0:T(8,128)(2,1)S(1)} %get-tuple-element.14.low), custom_call_target="tpu_custom_call" | custom-call | flops 369098752 | bytes 524288 | tf_op jit(solution)/shard_map/pallas_call | solution.py:426
  7.4 17.5 %all_to_all.10.data = f32[160,2,128]{2,1,0:T(2,128)S(1)} all-to-all(f32[160,2,128]{2,1,0:T(2,128)S(1)} %shard_map.75), channel_id=1, replica_groups=mesh['cuts'=4,'group'=8] {'cuts','group'}, dimensions={0} | all-to-all | bytes 327680 | tf_op jit(solution)/shard_map/all_to_all | solution.py:531
  24.9 0.3 shard_map.76
  25.2 11.2 %all_to_all.11.fields = f32[96,4,128]{2,1,0:T(4,128)S(1)} all-to-all(f32[96,4,128]{2,1,0:T(4,128)S(1)} %shard_map.76), channel_id=1, replica_groups=mesh['cuts'=4,'group'=8] {'cuts','group'}, dimensions={0} | all-to-all | bytes 393216 | tf_op jit(solution)/shard_map/all_to_all | solution.py:536
  36.4 0.8 %shard_map.77 = (f32[2,128,128]{2,1,0:T(8,128)S(1)}, f32[96,128]{1,0:T(8,128)S(1)}) custom-call(f32[96,4,128]{2,1,0:T(4,128)S(1)} %all_to_all.11.fields), custom_call_target="tpu_custom_call" | custom-call | flops 268435456 | bytes 524288 | tf_op jit(solution)/shard_map/pallas_call | solution.py:426
  37.2 0.1 collective-permute-start.1
  37.3 3.5 %collective-permute-done.1.state = f32[96,128]{1,0:T(8,128)S(1)} collective-permute-done((f32[96,128]{1,0:T(8,128)S(1)}, f32[96,128]{1,0:T(8,128)S(1)}, u32[]{:S(2)}, u32[]{:S(2)}) %collective-permute-start.1) | collective-permute-done | bytes 49184 | tf_op jit(solution)/shard_map/ppermute | solution.py:545
  40.8 2.4 %shard_map.79 = f32[2,128,128]{2,1,0:T(8,128)} custom-call(f32[2,128,128]{2,1,0:T(8,128)S(1)} %shard_map.78.field, f32[96,128]{1,0:T(8,128)S(1)} %collective-permute-done.1.state, bf16[256,256]{1,0:T(8,128)(2,1)S(1)} %get-tuple-element.13.high, bf16[256,256]{1,0:T(8,128)(2,1)S(1)} %get-tuple-element.14.low), custom_call_target="tpu_custom_call" | custom-call | flops 637534208 | bytes 524288 | tf_op jit(solution)/shard_map/pallas_call | solution.py:426
  (2 shorter events, 0.0 us)
Async XLA Ops:
  0.0 1.9 %copy-start = (f32[1,2,128,128]{3,2,1,0:T(8,128)S(1)}, f32[1,2,128,128]{3,2,1,0:T(8,128)}, u32[]{:S(2)}) copy-start(f32[1,2,128,128]{3,2,1,0:T(8,128)} %param.7) | copy-start | bytes 393220
  0.0 1.9 %copy-start.1 = (f32[2,128,128]{2,1,0:T(8,128)S(1)}, f32[2,128,128]{2,1,0:T(8,128)}, u32[]{:S(2)}) copy-start(f32[2,128,128]{2,1,0:T(8,128)} %propagator.1) | copy-start | bytes 393220
  1.5 4.3 %collective-permute-start = (f32[64,128]{1,0:T(8,128)S(1)}, f32[64,128]{1,0:T(8,128)S(1)}, u32[]{:S(2)}, u32[]{:S(2)}) collective-permute-start(f32[64,128]{1,0:T(8,128)S(1)} %shard_map.73.state), channel_id=1, source_target_pairs={{1,0},{2,1},{3,2},{4,3},{5,4},{6,5},{7,6},{8,7},{9,8},{10,9},{11,1... | collective-permute-start | bytes 98312 | tf_op jit(solution)/shard_map/ppermute | solution.py:506
  1.9 0.7 %copy-start.2 = (f32[2,32]{1,0:T(2,128)S(1)}, f32[2,32]{1,0:T(2,128)}, u32[]{:S(2)}) copy-start(f32[2,32]{1,0:T(2,128)} %rest_0_.1) | copy-start | bytes 772
  37.2 3.6 %collective-permute-start.1 = (f32[96,128]{1,0:T(8,128)S(1)}, f32[96,128]{1,0:T(8,128)S(1)}, u32[]{:S(2)}, u32[]{:S(2)}) collective-permute-start(f32[96,128]{1,0:T(8,128)S(1)} %get-tuple-element.16.state), channel_id=1, source_target_pairs={{1,0},{2,1},{3,2},{4,3},{5,4},{6,5},{7,6},{8,7},{9,8},{10,9},{11,1... | collective-permute-start | bytes 147464 | tf_op jit(solution)/shard_map/ppermute | solution.py:545

commit v8 on v6

--- a/solution.py
+++ b/solution.py
@@ -155,10 +155,15 @@
         where = slice(start * size, (start + width) * size)
         if not filled:
             hot_ref[:, where] = one_hot(place, start, width, 2 * grid)
-        col_hit = hits(lanes(col, start, width), half)
+        col_ids = lanes(col, start, width).astype(F32)
+        col_rows = lax.broadcasted_iota(jnp.int32, (half, col_ids.shape[1]), 0).astype(F32)
+        if half <= 256:
+            col_ids, col_rows = col_ids.astype(BF16), col_rows.astype(BF16)
+        col_hit = col_rows == col_ids
         for part, weight in ((0, weight_real), (1, weight_imag)):
-            value = jnp.where(col_hit, lanes(weight, start, width), 0.0)
-            spread_ref[part * half : (part + 1) * half, where] = value.astype(BF16)
+            value = lanes(weight, start, width).astype(BF16)
+            value = jnp.where(col_hit, value, jnp.zeros((), BF16))
+            spread_ref[part * half : (part + 1) * half, where] = value
     span = blocks * size
     source = dot(hot_ref[:, :span], spread_ref[:, :span], 1, 1)
     source_real, source_imag = fold(source[:grid], source[grid:])

time: 43.3 us -> 43.3 us (level)
  no operation moved by 1% of the time
where the time goes in v8:
time: 43.3 us; the launch traced here: 43.1 us
  blocking collectives  28.7 us (66%)
  Pallas kernels  7.79 us (18%)
  waiting for transfers between devices  5.46 us (13%)
  local copies, waits for them, and re-layouts  0.66 us (2%)
    all_to_all x1, blocking collectives, on_device(): data = lax.all_to_all(field, AXES, split_axis=0, concat_axis=0, tiled=True)  17.5 us
    all_to_all x1, blocking collectives, on_device(): fields = lax.all_to_all(sent, AXES, split_axis=0, concat_axis=0, tiled=True)  11.2 us
    pallas_call x7, Pallas kernels, call(): pl.pallas_call(kernel, out_shape=out_shape, in_specs=specs, out_specs=jax...  7.79 us
    ppermute x2, waiting for transfers between devices, on_device(): behind = lax.ppermute(state, AXES, route)  5.46 us
  transfers between devices with their start and end apart: 2, of which 2 were waited for; matrix products, arithmetic and copies ran while one was open for 1% of the time, Pallas kernels for 3%

profile of v8, /device:TPU:1, one launch (start us, length us, event | category | flops | bytes accessed | tf_op | source)
XLA Modules:
  0.0 43.1 jit_solution(4986172783539932769)
XLA Ops:
  0.0 0.0 copy-start
  0.0 0.0 copy-start.1
  0.0 1.5 %shard_map.73.state = f32[64,128]{1,0:T(8,128)S(1)} custom-call(f32[2,128,128]{2,1,0:T(8,128)} %bitcast.5, f32[16,128]{1,0:T(8,128)} %bitcast.7, f32[16,128]{1,0:T(8,128)} %bitcast.8, s32[16,128]{1,0:T(8,128)} %bitcast.9, s32[1,16]{1,0:T(1,128)} %dest_hbm.1), custom_call_target="tpu_custom_call" | custom-call | flops 134217728 | bytes 524288 | tf_op jit(solution)/shard_map/pallas_call | solution.py:431
  1.5 0.1 collective-permute-start
  1.6 0.2 sine_multiply_fusion
  1.8 0.1 fusion.13.rest_3_
  1.9 0.0 copy-start.2
  1.9 0.0 copy-done
  1.9 0.0 copy-done.1
  1.9 0.7 %copy-done.2 = f32[2,32]{1,0:T(2,128)S(1)} copy-done((f32[2,32]{1,0:T(2,128)S(1)}, f32[2,32]{1,0:T(2,128)}, u32[]{:S(2)}) %copy-start.2) | copy-done | bytes 280
  2.6 1.2 %shard_map.74 = (f32[2,128,128]{2,1,0:T(8,128)S(1)}, bf16[256,256]{1,0:T(8,128)(2,1)S(1)}, bf16[256,256]{1,0:T(8,128)(2,1)S(1)}, bf16[64,192]{1,0:T(8,128)(2,1)S(1)}) custom-call(f32[2,128,128]{2,1,0:T(8,128)S(1)} %bitcast.6, f32[64,128]{1,0:T(8,128)S(1)} %shard_map.73.state, f32[2,128,128]{2,1,0:T(8,128)S(1)} %copy-done.1, f32[2,32]{1,0:T(2,128)S(1)} %copy-done.2, ...), custom_call_target="tpu_custom_call" | custom-call | flops 234881024 | bytes 524288 | tf_op jit(solution)/shard_map/pallas_call | solution.py:431
  3.8 2.0 %collective-permute-done.state = f32[64,128]{1,0:T(8,128)S(1)} collective-permute-done((f32[64,128]{1,0:T(8,128)S(1)}, f32[64,128]{1,0:T(8,128)S(1)}, u32[]{:S(2)}, u32[]{:S(2)}) %collective-permute-start) | collective-permute-done | bytes 32800 | tf_op jit(solution)/shard_map/ppermute | solution.py:511
  5.8 1.6 %shard_map.75 = f32[160,2,128]{2,1,0:T(2,128)S(1)} custom-call(f32[2,128,128]{2,1,0:T(8,128)S(1)} %get-tuple-element.12.field, f32[64,128]{1,0:T(8,128)S(1)} %collective-permute-done.state, bf16[256,256]{1,0:T(8,128)(2,1)S(1)} %get-tuple-element.13.high, bf16[256,256]{1,0:T(8,128)(2,1)S(1)} %get-tuple-element.14.low), custom_call_target="tpu_custom_call" | custom-call | flops 369098752 | bytes 524288 | tf_op jit(solution)/shard_map/pallas_call | solution.py:431
  7.4 17.5 %all_to_all.10.data = f32[160,2,128]{2,1,0:T(2,128)S(1)} all-to-all(f32[160,2,128]{2,1,0:T(2,128)S(1)} %shard_map.75), channel_id=1, replica_groups=mesh['cuts'=4,'group'=8] {'cuts','group'}, dimensions={0} | all-to-all | bytes 327680 | tf_op jit(solution)/shard_map/all_to_all | solution.py:536
  24.9 0.3 shard_map.76
  25.2 11.2 %all_to_all.11.fields = f32[96,4,128]{2,1,0:T(4,128)S(1)} all-to-all(f32[96,4,128]{2,1,0:T(4,128)S(1)} %shard_map.76), channel_id=1, replica_groups=mesh['cuts'=4,'group'=8] {'cuts','group'}, dimensions={0} | all-to-all | bytes 393216 | tf_op jit(solution)/shard_map/all_to_all | solution.py:541
  36.4 0.8 %shard_map.77 = (f32[2,128,128]{2,1,0:T(8,128)S(1)}, f32[96,128]{1,0:T(8,128)S(1)}) custom-call(f32[96,4,128]{2,1,0:T(4,128)S(1)} %all_to_all.11.fields), custom_call_target="tpu_custom_call" | custom-call | flops 268435456 | bytes 524288 | tf_op jit(solution)/shard_map/pallas_call | solution.py:431
  37.2 0.1 collective-permute-start.1
  37.3 3.5 %collective-permute-done.1.state = f32[96,128]{1,0:T(8,128)S(1)} collective-permute-done((f32[96,128]{1,0:T(8,128)S(1)}, f32[96,128]{1,0:T(8,128)S(1)}, u32[]{:S(2)}, u32[]{:S(2)}) %collective-permute-start.1) | collective-permute-done | bytes 49184 | tf_op jit(solution)/shard_map/ppermute | solution.py:550
  40.8 2.4 %shard_map.79 = f32[2,128,128]{2,1,0:T(8,128)} custom-call(f32[2,128,128]{2,1,0:T(8,128)S(1)} %shard_map.78.field, f32[96,128]{1,0:T(8,128)S(1)} %collective-permute-done.1.state, bf16[256,256]{1,0:T(8,128)(2,1)S(1)} %get-tuple-element.13.high, bf16[256,256]{1,0:T(8,128)(2,1)S(1)} %get-tuple-element.14.low), custom_call_target="tpu_custom_call" | custom-call | flops 637534208 | bytes 524288 | tf_op jit(solution)/shard_map/pallas_call | solution.py:431
  (2 shorter events, 0.0 us)
Async XLA Ops:
  0.0 1.9 %copy-start = (f32[1,2,128,128]{3,2,1,0:T(8,128)S(1)}, f32[1,2,128,128]{3,2,1,0:T(8,128)}, u32[]{:S(2)}) copy-start(f32[1,2,128,128]{3,2,1,0:T(8,128)} %param.7) | copy-start | bytes 393220
  0.0 1.9 %copy-start.1 = (f32[2,128,128]{2,1,0:T(8,128)S(1)}, f32[2,128,128]{2,1,0:T(8,128)}, u32[]{:S(2)}) copy-start(f32[2,128,128]{2,1,0:T(8,128)} %propagator.1) | copy-start | bytes 393220
  1.5 4.3 %collective-permute-start = (f32[64,128]{1,0:T(8,128)S(1)}, f32[64,128]{1,0:T(8,128)S(1)}, u32[]{:S(2)}, u32[]{:S(2)}) collective-permute-start(f32[64,128]{1,0:T(8,128)S(1)} %shard_map.73.state), channel_id=1, source_target_pairs={{1,0},{2,1},{3,2},{4,3},{5,4},{6,5},{7,6},{8,7},{9,8},{10,9},{11,1... | collective-permute-start | bytes 98312 | tf_op jit(solution)/shard_map/ppermute | solution.py:511
  1.9 0.7 %copy-start.2 = (f32[2,32]{1,0:T(2,128)S(1)}, f32[2,32]{1,0:T(2,128)}, u32[]{:S(2)}) copy-start(f32[2,32]{1,0:T(2,128)} %rest_0_.1) | copy-start | bytes 772
  37.2 3.6 %collective-permute-start.1 = (f32[96,128]{1,0:T(8,128)S(1)}, f32[96,128]{1,0:T(8,128)S(1)}, u32[]{:S(2)}, u32[]{:S(2)}) collective-permute-start(f32[96,128]{1,0:T(8,128)S(1)} %get-tuple-element.16.state), channel_id=1, source_target_pairs={{1,0},{2,1},{3,2},{4,3},{5,4},{6,5},{7,6},{8,7},{9,8},{10,9},{11,1... | collective-permute-start | bytes 147464 | tf_op jit(solution)/shard_map/ppermute | solution.py:550

commit v9 on v6

--- a/solution.py
+++ b/solution.py
@@ -42,14 +42,16 @@
         ],
         axis=0,
     )
-    return split(form)
+    return split(jnp.concatenate([form, form.T], axis=0))
 
 
 def diffract(real, imag, form_high, form_low):
     size = real.shape[0]
     high, low = split(jnp.concatenate([real, imag], axis=1))
-    both = dot(jnp.concatenate([high, low], axis=0), form_high, 1, 1)
-    right = both[:size] + both[size:] + dot(high, form_low, 1, 1)
+    form_high, turned_high = form_high[: 2 * size], form_high[2 * size :]
+    form_low, turned_low = form_low[: 2 * size], form_low[2 * size :]
+    both = dot(jnp.concatenate([high, low], axis=0), turned_high, 1, 0)
+    right = both[:size] + both[size:] + dot(high, turned_low, 1, 0)
     high, low = split(jnp.concatenate([right[:, :size], right[:, size:]], axis=0))
     both = dot(form_high, jnp.concatenate([high, low], axis=1), 1, 0)
     out = both[:, :size] + both[:, size:] + dot(form_low, high, 1, 0)
@@ -504,7 +506,7 @@
     )
     route = [((i + 1) % count, i) for i in range(count)]
     behind = lax.ppermute(state, AXES, route)
-    form_shape = jax.ShapeDtypeStruct((2 * grid, 2 * grid), BF16)
+    form_shape = jax.ShapeDtypeStruct((4 * grid, 2 * grid), BF16)
     made = [shape(2, grid, grid), form_shape, form_shape]
     tables = ()
     if rows:

time: 43.3 us -> 43.3 us (level)
  no operation moved by 1% of the time
where the time goes in v9:
time: 43.3 us; the launch traced here: 43.1 us
  blocking collectives  28.7 us (66%)
  Pallas kernels  7.83 us (18%)
  waiting for transfers between devices  5.42 us (13%)
  local copies, waits for them, and re-layouts  0.66 us (2%)
    all_to_all x1, blocking collectives, on_device(): data = lax.all_to_all(field, AXES, split_axis=0, concat_axis=0, tiled=True)  17.5 us
    all_to_all x1, blocking collectives, on_device(): fields = lax.all_to_all(sent, AXES, split_axis=0, concat_axis=0, tiled=True)  11.2 us
    pallas_call x7, Pallas kernels, call(): pl.pallas_call(kernel, out_shape=out_shape, in_specs=specs, out_specs=jax...  7.83 us
    ppermute x2, waiting for transfers between devices, on_device(): behind = lax.ppermute(state, AXES, route)  5.42 us
  transfers between devices with their start and end apart: 2, of which 2 were waited for; matrix products, arithmetic and copies ran while one was open for 1% of the time, Pallas kernels for 3%

profile of v9, /device:TPU:1, one launch (start us, length us, event | category | flops | bytes accessed | tf_op | source)
XLA Modules:
  0.0 43.1 jit_solution(17747570585802430323)
XLA Ops:
  0.0 0.0 copy-start
  0.0 0.0 copy-start.1
  0.0 1.5 %shard_map.73.state = f32[64,128]{1,0:T(8,128)S(1)} custom-call(f32[2,128,128]{2,1,0:T(8,128)} %bitcast.5, f32[16,128]{1,0:T(8,128)} %bitcast.7, f32[16,128]{1,0:T(8,128)} %bitcast.8, s32[16,128]{1,0:T(8,128)} %bitcast.9, s32[1,16]{1,0:T(1,128)} %dest_hbm.1), custom_call_target="tpu_custom_call" | custom-call | flops 134217728 | bytes 524288 | tf_op jit(solution)/shard_map/pallas_call | solution.py:428
  1.5 0.1 collective-permute-start
  1.6 0.2 sine_multiply_fusion
  1.8 0.1 fusion.13.rest_3_
  1.9 0.0 copy-start.2
  1.9 0.0 copy-done
  1.9 0.0 copy-done.1
  1.9 0.7 %copy-done.2 = f32[2,32]{1,0:T(2,128)S(1)} copy-done((f32[2,32]{1,0:T(2,128)S(1)}, f32[2,32]{1,0:T(2,128)}, u32[]{:S(2)}) %copy-start.2) | copy-done | bytes 280
  2.6 1.2 %shard_map.74 = (f32[2,128,128]{2,1,0:T(8,128)S(1)}, bf16[512,256]{1,0:T(8,128)(2,1)S(1)}, bf16[512,256]{1,0:T(8,128)(2,1)S(1)}, bf16[64,192]{1,0:T(8,128)(2,1)S(1)}) custom-call(f32[2,128,128]{2,1,0:T(8,128)S(1)} %bitcast.6, f32[64,128]{1,0:T(8,128)S(1)} %shard_map.73.state, f32[2,128,128]{2,1,0:T(8,128)S(1)} %copy-done.1, f32[2,32]{1,0:T(2,128)S(1)} %copy-done.2, ...), custom_call_target="tpu_custom_call" | custom-call | flops 234881024 | bytes 524288 | tf_op jit(solution)/shard_map/pallas_call | solution.py:428
  3.8 2.0 %collective-permute-done.state = f32[64,128]{1,0:T(8,128)S(1)} collective-permute-done((f32[64,128]{1,0:T(8,128)S(1)}, f32[64,128]{1,0:T(8,128)S(1)}, u32[]{:S(2)}, u32[]{:S(2)}) %collective-permute-start) | collective-permute-done | bytes 32800 | tf_op jit(solution)/shard_map/ppermute | solution.py:508
  5.8 1.6 %shard_map.75 = f32[160,2,128]{2,1,0:T(2,128)S(1)} custom-call(f32[2,128,128]{2,1,0:T(8,128)S(1)} %get-tuple-element.12.field, f32[64,128]{1,0:T(8,128)S(1)} %collective-permute-done.state, bf16[512,256]{1,0:T(8,128)(2,1)S(1)} %get-tuple-element.13.high, bf16[512,256]{1,0:T(8,128)(2,1)S(1)} %get-tuple-element.14.low), custom_call_target="tpu_custom_call" | custom-call | flops 369098752 | bytes 524288 | tf_op jit(solution)/shard_map/pallas_call | solution.py:428
  7.4 17.5 %all_to_all.10.data = f32[160,2,128]{2,1,0:T(2,128)S(1)} all-to-all(f32[160,2,128]{2,1,0:T(2,128)S(1)} %shard_map.75), channel_id=1, replica_groups=mesh['cuts'=4,'group'=8] {'cuts','group'}, dimensions={0} | all-to-all | bytes 327680 | tf_op jit(solution)/shard_map/all_to_all | solution.py:533
  24.9 0.3 shard_map.76
  25.2 11.2 %all_to_all.11.fields = f32[96,4,128]{2,1,0:T(4,128)S(1)} all-to-all(f32[96,4,128]{2,1,0:T(4,128)S(1)} %shard_map.76), channel_id=1, replica_groups=mesh['cuts'=4,'group'=8] {'cuts','group'}, dimensions={0} | all-to-all | bytes 393216 | tf_op jit(solution)/shard_map/all_to_all | solution.py:538
  36.4 0.8 %shard_map.77 = (f32[2,128,128]{2,1,0:T(8,128)S(1)}, f32[96,128]{1,0:T(8,128)S(1)}) custom-call(f32[96,4,128]{2,1,0:T(4,128)S(1)} %all_to_all.11.fields), custom_call_target="tpu_custom_call" | custom-call | flops 268435456 | bytes 524288 | tf_op jit(solution)/shard_map/pallas_call | solution.py:428
  37.2 0.1 collective-permute-start.1
  37.3 3.5 %collective-permute-done.1.state = f32[96,128]{1,0:T(8,128)S(1)} collective-permute-done((f32[96,128]{1,0:T(8,128)S(1)}, f32[96,128]{1,0:T(8,128)S(1)}, u32[]{:S(2)}, u32[]{:S(2)}) %collective-permute-start.1) | collective-permute-done | bytes 49184 | tf_op jit(solution)/shard_map/ppermute | solution.py:547
  40.8 2.4 %shard_map.79 = f32[2,128,128]{2,1,0:T(8,128)} custom-call(f32[2,128,128]{2,1,0:T(8,128)S(1)} %shard_map.78.field, f32[96,128]{1,0:T(8,128)S(1)} %collective-permute-done.1.state, bf16[512,256]{1,0:T(8,128)(2,1)S(1)} %get-tuple-element.13.high, bf16[512,256]{1,0:T(8,128)(2,1)S(1)} %get-tuple-element.14.low), custom_call_target="tpu_custom_call" | custom-call | flops 637534208 | bytes 524288 | tf_op jit(solution)/shard_map/pallas_call | solution.py:428
  (2 shorter events, 0.0 us)
Async XLA Ops:
  0.0 1.9 %copy-start = (f32[1,2,128,128]{3,2,1,0:T(8,128)S(1)}, f32[1,2,128,128]{3,2,1,0:T(8,128)}, u32[]{:S(2)}) copy-start(f32[1,2,128,128]{3,2,1,0:T(8,128)} %param.7) | copy-start | bytes 393220
  0.0 1.9 %copy-start.1 = (f32[2,128,128]{2,1,0:T(8,128)S(1)}, f32[2,128,128]{2,1,0:T(8,128)}, u32[]{:S(2)}) copy-start(f32[2,128,128]{2,1,0:T(8,128)} %propagator.1) | copy-start | bytes 393220
  1.5 4.3 %collective-permute-start = (f32[64,128]{1,0:T(8,128)S(1)}, f32[64,128]{1,0:T(8,128)S(1)}, u32[]{:S(2)}, u32[]{:S(2)}) collective-permute-start(f32[64,128]{1,0:T(8,128)S(1)} %shard_map.73.state), channel_id=1, source_target_pairs={{1,0},{2,1},{3,2},{4,3},{5,4},{6,5},{7,6},{8,7},{9,8},{10,9},{11,1... | collective-permute-start | bytes 98312 | tf_op jit(solution)/shard_map/ppermute | solution.py:508
  1.9 0.7 %copy-start.2 = (f32[2,32]{1,0:T(2,128)S(1)}, f32[2,32]{1,0:T(2,128)}, u32[]{:S(2)}) copy-start(f32[2,32]{1,0:T(2,128)} %rest_0_.1) | copy-start | bytes 772
  37.2 3.6 %collective-permute-start.1 = (f32[96,128]{1,0:T(8,128)S(1)}, f32[96,128]{1,0:T(8,128)S(1)}, u32[]{:S(2)}, u32[]{:S(2)}) collective-permute-start(f32[96,128]{1,0:T(8,128)S(1)} %get-tuple-element.16.state), channel_id=1, source_target_pairs={{1,0},{2,1},{3,2},{4,3},{5,4},{6,5},{7,6},{8,7},{9,8},{10,9},{11,1... | collective-permute-start | bytes 147464 | tf_op jit(solution)/shard_map/ppermute | solution.py:547

commit v10 on v6

--- a/solution.py
+++ b/solution.py
@@ -177,7 +177,7 @@
     blocks, size = phases.shape
     pairs = ((pixels_hbm, pixels), (phases_hbm, phases), (energy_hbm, energy), (dest_hbm, dest), (field_hbm, field))
     copies = [pltpu.make_async_copy(source, target, sems.at[k]) for k, (source, target) in enumerate(pairs)]
-    for copy in copies:
+    for copy in reversed(copies):
         copy.start()
     for copy in copies[:-1]:
         copy.wait()

time: 43.3 us -> 43.4 us (level)
  no operation moved by 1% of the time
where the time goes in v10:
time: 43.4 us; the launch traced here: 43.1 us
  blocking collectives  28.7 us (66%)
  Pallas kernels  7.77 us (18%)
  waiting for transfers between devices  5.48 us (13%)
  local copies, waits for them, and re-layouts  0.66 us (2%)
    all_to_all x1, blocking collectives, on_device(): data = lax.all_to_all(field, AXES, split_axis=0, concat_axis=0, tiled=True)  17.5 us
    all_to_all x1, blocking collectives, on_device(): fields = lax.all_to_all(sent, AXES, split_axis=0, concat_axis=0, tiled=True)  11.2 us
    pallas_call x7, Pallas kernels, call(): pl.pallas_call(kernel, out_shape=out_shape, in_specs=specs, out_specs=jax...  7.77 us
    ppermute x2, waiting for transfers between devices, on_device(): behind = lax.ppermute(state, AXES, route)  5.48 us
  transfers between devices with their start and end apart: 2, of which 2 were waited for; matrix products, arithmetic and copies ran while one was open for 1% of the time, Pallas kernels for 3%

profile of v10, /device:TPU:1, one launch (start us, length us, event | category | flops | bytes accessed | tf_op | source)
XLA Modules:
  0.0 43.1 jit_solution(7121962557368375476)
XLA Ops:
  0.0 0.0 copy-start
  0.0 0.0 copy-start.1
  0.0 1.5 %shard_map.73.state = f32[64,128]{1,0:T(8,128)S(1)} custom-call(f32[2,128,128]{2,1,0:T(8,128)} %bitcast.5, f32[16,128]{1,0:T(8,128)} %bitcast.7, f32[16,128]{1,0:T(8,128)} %bitcast.8, s32[16,128]{1,0:T(8,128)} %bitcast.9, s32[1,16]{1,0:T(1,128)} %dest_hbm.1), custom_call_target="tpu_custom_call" | custom-call | flops 134217728 | bytes 524288 | tf_op jit(solution)/shard_map/pallas_call | solution.py:426
  1.5 0.1 collective-permute-start
  1.6 0.2 sine_multiply_fusion
  1.8 0.1 fusion.13.rest_3_
  1.9 0.0 copy-start.2
  1.9 0.0 copy-done
  1.9 0.0 copy-done.1
  1.9 0.7 %copy-done.2 = f32[2,32]{1,0:T(2,128)S(1)} copy-done((f32[2,32]{1,0:T(2,128)S(1)}, f32[2,32]{1,0:T(2,128)}, u32[]{:S(2)}) %copy-start.2) | copy-done | bytes 280
  2.5 1.2 %shard_map.74 = (f32[2,128,128]{2,1,0:T(8,128)S(1)}, bf16[256,256]{1,0:T(8,128)(2,1)S(1)}, bf16[256,256]{1,0:T(8,128)(2,1)S(1)}, bf16[64,192]{1,0:T(8,128)(2,1)S(1)}) custom-call(f32[2,128,128]{2,1,0:T(8,128)S(1)} %bitcast.6, f32[64,128]{1,0:T(8,128)S(1)} %shard_map.73.state, f32[2,128,128]{2,1,0:T(8,128)S(1)} %copy-done.1, f32[2,32]{1,0:T(2,128)S(1)} %copy-done.2, ...), custom_call_target="tpu_custom_call" | custom-call | flops 234881024 | bytes 524288 | tf_op jit(solution)/shard_map/pallas_call | solution.py:426
  3.7 2.0 %collective-permute-done.state = f32[64,128]{1,0:T(8,128)S(1)} collective-permute-done((f32[64,128]{1,0:T(8,128)S(1)}, f32[64,128]{1,0:T(8,128)S(1)}, u32[]{:S(2)}, u32[]{:S(2)}) %collective-permute-start) | collective-permute-done | bytes 32800 | tf_op jit(solution)/shard_map/ppermute | solution.py:506
  5.7 1.6 %shard_map.75 = f32[160,2,128]{2,1,0:T(2,128)S(1)} custom-call(f32[2,128,128]{2,1,0:T(8,128)S(1)} %get-tuple-element.12.field, f32[64,128]{1,0:T(8,128)S(1)} %collective-permute-done.state, bf16[256,256]{1,0:T(8,128)(2,1)S(1)} %get-tuple-element.13.high, bf16[256,256]{1,0:T(8,128)(2,1)S(1)} %get-tuple-element.14.low), custom_call_target="tpu_custom_call" | custom-call | flops 369098752 | bytes 524288 | tf_op jit(solution)/shard_map/pallas_call | solution.py:426
  7.4 17.5 %all_to_all.10.data = f32[160,2,128]{2,1,0:T(2,128)S(1)} all-to-all(f32[160,2,128]{2,1,0:T(2,128)S(1)} %shard_map.75), channel_id=1, replica_groups=mesh['cuts'=4,'group'=8] {'cuts','group'}, dimensions={0} | all-to-all | bytes 327680 | tf_op jit(solution)/shard_map/all_to_all | solution.py:531
  24.9 0.3 shard_map.76
  25.2 11.2 %all_to_all.11.fields = f32[96,4,128]{2,1,0:T(4,128)S(1)} all-to-all(f32[96,4,128]{2,1,0:T(4,128)S(1)} %shard_map.76), channel_id=1, replica_groups=mesh['cuts'=4,'group'=8] {'cuts','group'}, dimensions={0} | all-to-all | bytes 393216 | tf_op jit(solution)/shard_map/all_to_all | solution.py:536
  36.4 0.8 %shard_map.77 = (f32[2,128,128]{2,1,0:T(8,128)S(1)}, f32[96,128]{1,0:T(8,128)S(1)}) custom-call(f32[96,4,128]{2,1,0:T(4,128)S(1)} %all_to_all.11.fields), custom_call_target="tpu_custom_call" | custom-call | flops 268435456 | bytes 524288 | tf_op jit(solution)/shard_map/pallas_call | solution.py:426
  37.2 0.1 collective-permute-start.1
  37.3 3.5 %collective-permute-done.1.state = f32[96,128]{1,0:T(8,128)S(1)} collective-permute-done((f32[96,128]{1,0:T(8,128)S(1)}, f32[96,128]{1,0:T(8,128)S(1)}, u32[]{:S(2)}, u32[]{:S(2)}) %collective-permute-start.1) | collective-permute-done | bytes 49184 | tf_op jit(solution)/shard_map/ppermute | solution.py:545
  40.7 2.4 %shard_map.79 = f32[2,128,128]{2,1,0:T(8,128)} custom-call(f32[2,128,128]{2,1,0:T(8,128)S(1)} %shard_map.78.field, f32[96,128]{1,0:T(8,128)S(1)} %collective-permute-done.1.state, bf16[256,256]{1,0:T(8,128)(2,1)S(1)} %get-tuple-element.13.high, bf16[256,256]{1,0:T(8,128)(2,1)S(1)} %get-tuple-element.14.low), custom_call_target="tpu_custom_call" | custom-call | flops 637534208 | bytes 524288 | tf_op jit(solution)/shard_map/pallas_call | solution.py:426
  (2 shorter events, 0.0 us)
Async XLA Ops:
  0.0 1.9 %copy-start = (f32[1,2,128,128]{3,2,1,0:T(8,128)S(1)}, f32[1,2,128,128]{3,2,1,0:T(8,128)}, u32[]{:S(2)}) copy-start(f32[1,2,128,128]{3,2,1,0:T(8,128)} %param.7) | copy-start | bytes 393220
  0.0 1.9 %copy-start.1 = (f32[2,128,128]{2,1,0:T(8,128)S(1)}, f32[2,128,128]{2,1,0:T(8,128)}, u32[]{:S(2)}) copy-start(f32[2,128,128]{2,1,0:T(8,128)} %propagator.1) | copy-start | bytes 393220
  1.5 4.2 %collective-permute-start = (f32[64,128]{1,0:T(8,128)S(1)}, f32[64,128]{1,0:T(8,128)S(1)}, u32[]{:S(2)}, u32[]{:S(2)}) collective-permute-start(f32[64,128]{1,0:T(8,128)S(1)} %shard_map.73.state), channel_id=1, source_target_pairs={{1,0},{2,1},{3,2},{4,3},{5,4},{6,5},{7,6},{8,7},{9,8},{10,9},{11,1... | collective-permute-start | bytes 98312 | tf_op jit(solution)/shard_map/ppermute | solution.py:506
  1.9 0.7 %copy-start.2 = (f32[2,32]{1,0:T(2,128)S(1)}, f32[2,32]{1,0:T(2,128)}, u32[]{:S(2)}) copy-start(f32[2,32]{1,0:T(2,128)} %rest_0_.1) | copy-start | bytes 772
  37.2 3.6 %collective-permute-start.1 = (f32[96,128]{1,0:T(8,128)S(1)}, f32[96,128]{1,0:T(8,128)S(1)}, u32[]{:S(2)}, u32[]{:S(2)}) collective-permute-start(f32[96,128]{1,0:T(8,128)S(1)} %get-tuple-element.16.state), channel_id=1, source_target_pairs={{1,0},{2,1},{3,2},{4,3},{5,4},{6,5},{7,6},{8,7},{9,8},{10,9},{11,1... | collective-permute-start | bytes 147464 | tf_op jit(solution)/shard_map/ppermute | solution.py:545
